TPU v7x, 512 devices: a whole 4x8x8 slice. The times are simulated.
512 devices in a mesh: gx: 16 (over y, core), gy: 32 (over z, x).
Axes of the slice: x: 4, y: 8, z: 8, core: 2. Of those that a mesh axis runs over, the one named last changes fastest.
Arguments:
- concentration: float32 [2048, 4, 4, 4096], P('gx', None, None, 'gy'), may hold values from -6 to 6
- courant_x: float32 [2048, 4, 4096], P('gx', None, 'gy'), may hold values from 300 to 1200
- courant_y: float32 [2048, 4, 4096], P('gx', None, 'gy'), may hold values from -0.4 to 0.4
- vert_diff: float32 [2048, 4, 4096], P('gx', None, 'gy'), may hold values from 0.05 to 0.45
- emission: float32 [2048, 4, 4096], P('gx', None, 'gy'), may hold values from -6 to 6
- building: int32 [16, 32], P('gx', 'gy'), may hold values 0 or 1
Outputs:
- updated: float32 [2048, 4, 4, 4096], P('gx', None, None, 'gy')
Inputs may be any that keep to these rules, and one draw needn't show every extreme that they name: 1 marks a tile filled by a building, 0 a fluid tile.
All inputs are finite; a program needn't handle non-finite values. No bound on the sum of `building` on one device may be relied on, other than what follows from the above.
Results may differ from a plain program's by a relative error of at most 0.00002.
Values sent between devices are 32-bit elements; how exact they have to be, the bound alone decides.
No kernel may reach another device: no remote copies, remote signals or barrier semaphores. Data moves between devices by JAX's collectives and lax.ppermute only.
A program may use at most 64 MiB of HBM per device.

v0:
```python
import functools

import jax
import jax.numpy as jnp
from jax import lax
from jax.experimental import pallas as pl
from jax.experimental.pallas import tpu as pltpu
from jax.sharding import PartitionSpec as P

cross_diff = 300.0
span_diff = 0.25

SUB, LANE = 8, 128
VMEM = pl.BlockSpec(memory_space=pltpu.VMEM)
SMEM = pl.BlockSpec(memory_space=pltpu.SMEM)
LIMIT = 16 * 1024 * 1024


def sub_ids():
    return lax.broadcasted_iota(jnp.int32, (SUB, LANE), 0)


def lane_ids():
    return lax.broadcasted_iota(jnp.int32, (SUB, LANE), 1)


def lanes(x, shift):
    shift %= LANE
    return pltpu.roll(x, shift, 1) if shift else x


def subs(x, shift):
    shift %= SUB
    return pltpu.roll(x, shift, 0) if shift else x


def fluid_of(building_ref):
    return 1.0 - building_ref[0, 0].astype(jnp.float32)


def both_rows(pair):
    low = sub_ids() < 4
    turned = subs(pair, 4)
    return jnp.where(low, pair, turned), jnp.where(low, turned, pair)


def level_above(x):
    return jnp.where(sub_ids() % 4 == 3, 0.0, subs(x, -1))


def level_below(x):
    return jnp.where(sub_ids() % 4 == 0, 0.0, subs(x, 1))


def span_operator(q, left, right, wind):
    wind_pos = jnp.maximum(wind, 0.0)
    wind_neg = jnp.maximum(-wind, 0.0)
    return (wind_pos + span_diff) * (left - q) + (wind_neg + span_diff) * (right - q)


def side_of(q, left, right, wind, face, face_up, source, fluid):
    value = q + span_operator(q, left, right, wind)
    value = value + face * (level_below(q) - q) + face_up * (level_above(q) - q)
    return fluid * (value + source)


def pack_kernel(c_ref, cx_ref, cy_ref, vd_ref, em_ref, building_ref, a_ref, b_ref):
    lane, sub = lane_ids(), sub_ids()
    fluid = fluid_of(building_ref)
    low = sub < 4
    even_gy = lax.rem(lax.axis_index("gy"), 2) == 0
    quarter = lane // 4
    columns = []
    for half in range(2):
        picked = []
        for g in range(4):
            acc = jnp.zeros((SUB, LANE), jnp.float32)
            for m in range(32):
                acc = jnp.where(
                    quarter == m, lanes(c_ref[4 * m + g, 8 * half : 8 * half + 8, :], 4 * m + 2), acc
                )
            picked.append(acc)
        found = []
        for j in range(4):
            out = lanes(picked[0], -j)
            for g in range(1, 4):
                out = jnp.where(lane % 4 == g, lanes(picked[g], g - j), out)
            found.append(out)
        columns.append(found)
    even = lane % 2 == 0
    first, last = [], []
    for ref in (cx_ref, cy_ref, vd_ref, em_ref):
        acc = jnp.zeros((SUB, LANE), jnp.float32)
        for k in range(64):
            acc = jnp.where(lane // 2 == k, lanes(ref[k], 2 * k + 1), acc)
        turned = subs(acc, 4)
        at_even = jnp.where(low, acc, turned)
        at_odd = jnp.where(low, turned, acc)
        last.append(jnp.where(even, at_even, lanes(at_odd, 1)))
        first.append(jnp.where(even, lanes(at_even, -1), at_odd))
    sides = []
    for (outer, inner), coefs in (((2, 3), first), ((1, 0), last)):
        pull = fluid * (coefs[0] + cross_diff)
        sides.append(
            [
                columns[0][outer],
                columns[1][outer],
                columns[0][inner],
                columns[1][inner],
                jnp.where(low, pull, coefs[1]),
                jnp.where(low, coefs[2], coefs[3]),
            ]
        )
    for n in range(6):
        to_left, to_right = sides[0][n], sides[1][n]
        a_ref[n] = jnp.where(even_gy, to_right, to_left)
        b_ref[n] = jnp.where(even_gy, to_left, to_right)


def factor_kernel(cx_ref, building_ref, inv_ref, prod_ref, ends_ref):
    fluid = fluid_of(building_ref)
    push = cross_diff * fluid

    def rows(k, state):
        ratio, from_prev, chain, first_prev = state
        for u in range(4):
            for r, wind in enumerate(both_rows(cx_ref[4 * k + u])):
                row = 8 * k + 2 * u + r
                pull = fluid * (wind + cross_diff)
                inv = 1.0 / ((1.0 + pull + push) - pull * ratio)
                from_prev = pull * inv * from_prev
                first_prev = first_prev + chain * from_prev
                ratio = push * inv
                chain = chain * ratio
                inv_ref[row] = inv
                prod_ref[row] = from_prev
        return ratio, from_prev, chain, first_prev

    zero = jnp.zeros((SUB, LANE), jnp.float32)
    ratio, from_prev, chain, first_prev = lax.fori_loop(0, 16, rows, (zero, zero + 1.0, zero + 1.0, zero))
    low = sub_ids() < 4
    ends_ref[0] = jnp.where(low, first_prev, chain)
    ends_ref[1] = jnp.where(low, from_prev, ratio)


def ghost_column(q, left, right, pull, wind, face, emitted):
    lane, sub = lane_ids(), sub_ids()
    fluid = jnp.where(pull > 0.0, 1.0, 0.0)
    face_up = level_above(face)
    sources = [
        jnp.where(sub == 0, emitted, jnp.where(sub == 4, subs(emitted, -1), 0.0)),
        jnp.where(sub == 0, subs(emitted, -2), jnp.where(sub == 4, subs(emitted, -3), 0.0)),
    ]
    inv = 1.0 / (1.0 + pull + cross_diff * fluid)
    lower = pull * inv
    upper = cross_diff * fluid * inv
    sides = [
        inv * side_of(q[h], left[h], right[h], wind, face, face_up, sources[h], fluid) for h in range(2)
    ]
    sides.append(jnp.where(lane == 0, lower, 0.0))
    sides.append(jnp.where(lane == LANE - 1, upper, 0.0))
    lower = jnp.where(lane == 0, 0.0, lower)
    upper = jnp.where(lane == LANE - 1, 0.0, upper)
    step = 1
    while step < LANE:
        low_prev, up_prev = lanes(lower, step), lanes(upper, step)
        low_next, up_next = lanes(lower, -step), lanes(upper, -step)
        inv = 1.0 / (1.0 - lower * up_prev - upper * low_next)
        lower, upper, from_low, from_up = inv * lower * low_prev, inv * upper * up_next, inv * lower, inv * upper
        sides = [inv * s + from_low * lanes(s, step) + from_up * lanes(s, -step) for s in sides]
        step *= 2
    return sides


def side_kernel(
    c_ref, cx_ref, cy_ref, vd_ref, em_ref, inv_ref, ends_ref, building_ref,
    sent_a_ref, sent_b_ref, got_a_ref, got_b_ref,
    side_ref, partial_ref, ghost_ref, rows_ref,
):
    lane, sub = lane_ids(), sub_ids()
    low = sub < 4
    fluid = fluid_of(building_ref)
    push = cross_diff * fluid
    even_gy = lax.rem(lax.axis_index("gy"), 2) == 0
    own_left = [jnp.where(even_gy, sent_b_ref[n], sent_a_ref[n]) for n in range(2)]
    own_right = [jnp.where(even_gy, sent_a_ref[n], sent_b_ref[n]) for n in range(2)]
    from_left = [jnp.where(even_gy, got_b_ref[n], got_a_ref[n]) for n in range(6)]
    from_right = [jnp.where(even_gy, got_a_ref[n], got_b_ref[n]) for n in range(6)]

    extra = jnp.zeros((SUB, LANE), jnp.float32)
    for s, (got, own) in enumerate(((from_left, own_left), (from_right, own_right))):
        left, right = (got[2:4], own) if s == 0 else (own, got[2:4])
        pull, wind = both_rows(got[4])
        face, emitted = both_rows(got[5])
        parts = ghost_column(got[0:2], left, right, pull, wind, face, emitted)
        for n in range(4):
            ghost_ref[4 * s + n] = parts[n]
        ends = [
            (parts[0], 0), (parts[1], 0), (parts[0], 1), (parts[1], 1),
            (parts[2], 0), (parts[3], 0), (parts[2], 1), (parts[3], 1),
        ]
        for j, (part, tail) in enumerate(ends):
            extra = jnp.where(lane == 2 * j + s, lanes(part, 2 * j + s + tail), extra)

    def rows(k, state):
        west, east, last, first, chain = state
        for u in range(4):
            pair = 4 * k + u
            pulls = both_rows(cx_ref[pair])
            winds = both_rows(cy_ref[pair])
            faces = both_rows(vd_ref[pair])
            for r in range(2):
                row = 2 * pair + r
                face_up = level_above(faces[r])
                inv = inv_ref[row]
                from_last = fluid * (pulls[r] + cross_diff) * inv
                new_last, new_first = [], []
                for h in range(2):
                    q = c_ref[row, 8 * h : 8 * h + 8, :]
                    left = jnp.where(lane == 0, lanes(west[h], -(2 * u + r)), lanes(q, 1))
                    right = jnp.where(lane == LANE - 1, lanes(east[h], -(2 * u + r) - 1), lanes(q, -1))
                    low_tracer = em_ref[pair, 4 * r + 2 * h : 4 * r + 2 * h + 1, :]
                    high_tracer = em_ref[pair, 4 * r + 2 * h + 1 : 4 * r + 2 * h + 2, :]
                    source = jnp.where(sub == 0, low_tracer, jnp.where(sub == 4, high_tracer, 0.0))
                    side = side_of(q, left, right, winds[r], faces[r], face_up, source, fluid)
                    value = side * inv + from_last * last[h]
                    side_ref[row, 8 * h : 8 * h + 8, :] = side
                    partial_ref[row, 8 * h : 8 * h + 8, :] = value
                    new_last.append(value)
                    new_first.append(first[h] + chain * value)
                last, first = new_last, new_first
                chain = chain * (push * inv)
        west = [lanes(x, -8) for x in west]
        east = [lanes(x, -8) for x in east]
        return west, east, last, first, chain

    zero = jnp.zeros((SUB, LANE), jnp.float32)
    start = (from_left[0:2], from_right[0:2], [zero, zero], [zero, zero], zero + 1.0)
    _, _, last, first, _ = lax.fori_loop(0, 16, rows, start)
    rows_ref[0], rows_ref[1] = first
    rows_ref[2], rows_ref[3] = last
    rows_ref[4] = ends_ref[0]
    rows_ref[5] = ends_ref[1]
    rows_ref[6] = extra


def interface(blocks, place):
    zero = jnp.zeros((SUB, LANE), jnp.float32)
    own, slope = [zero, zero], zero
    kept_own, kept_slope = own, slope
    forms = []
    for k, (first, last, first_prev, first_next, last_prev, last_next) in enumerate(blocks):
        here = place == k
        kept_own = [jnp.where(here, own[h], kept_own[h]) for h in range(2)]
        kept_slope = jnp.where(here, slope, kept_slope)
        inv = 1.0 / (1.0 - first_prev * slope)
        start = [(first[h] + first_prev * own[h]) * inv for h in range(2)]
        start_next = first_next * inv
        forms.append((start, start_next))
        carried = last_prev * slope
        own = [last[h] + last_prev * own[h] + carried * start[h] for h in range(2)]
        slope = last_next + carried * start_next
    after = [zero, zero]
    following, mine = after, after
    for k in reversed(range(len(forms))):
        following = [jnp.where(place == k, after[h], following[h]) for h in range(2)]
        start, start_next = forms[k]
        after = [start[h] + start_next * after[h] for h in range(2)]
        mine = [jnp.where(place == k, after[h], mine[h]) for h in range(2)]
    preceding = [kept_own[h] + kept_slope * mine[h] for h in range(2)]
    return preceding, following


def finish_kernel(
    blocks, side_ref, partial_ref, cy_ref, vd_ref, inv_ref, prod_ref, ghost_ref, rows_ref, building_ref, out_ref
):
    lane = lane_ids()
    fluid = fluid_of(building_ref)
    push = cross_diff * fluid
    place = lax.axis_index("gx")
    main, extra = [], []
    for k in range(blocks):
        first_prev, first_next = both_rows(rows_ref[k, 4])
        last_prev, last_next = both_rows(rows_ref[k, 5])
        main.append(
            ([rows_ref[k, 0], rows_ref[k, 1]], [rows_ref[k, 2], rows_ref[k, 3]],
             first_prev, first_next, last_prev, last_next)
        )
        e = [lanes(rows_ref[k, 6], -2 * j) for j in range(8)]
        extra.append((e[0:2], e[2:4], e[4], e[5], e[6], e[7]))
    preceding, following = interface(main, place)
    ghost_prev, ghost_next = interface(extra, place)
    ghosts = []
    for s in range(2):
        ghosts.append(
            [
                ghost_ref[4 * s + h]
                + ghost_ref[4 * s + 2] * ghost_prev[h][:, s : s + 1]
                + ghost_ref[4 * s + 3] * ghost_next[h][:, s : s + 1]
                for h in range(2)
            ]
        )
    west = [lanes(x, 8) for x in ghosts[0]]
    east = [lanes(x, 8) for x in ghosts[1]]

    def rows(step, state):
        k = 15 - step
        west, east, after = state
        for u in reversed(range(4)):
            pair = 4 * k + u
            winds = both_rows(cy_ref[pair])
            faces = both_rows(vd_ref[pair])
            for r in reversed(range(2)):
                row = 2 * pair + r
                face = faces[r]
                face_up = level_above(face)
                inv = 1.0 / (1.0 + face + face_up)
                lower = jnp.where(sub_ids() % 4 == 0, 0.0, face * inv)
                upper = face_up * inv
                inv_near = 1.0 / (1.0 - lower * subs(upper, 1) - upper * subs(lower, -1))
                near_low, near_up = inv_near * lower, inv_near * upper
                far_low, far_up = near_low * subs(lower, 1), near_up * subs(upper, -1)
                inv_far = 1.0 / (1.0 - far_low * subs(far_up, 2) - far_up * subs(far_low, -2))
                scale = inv_far * inv_near
                far_low, far_up = inv_far * far_low, inv_far * far_up
                ratio = push * inv_ref[row]
                from_prev = prod_ref[row]
                for h in range(2):
                    at = slice(8 * h, 8 * h + 8)
                    star = partial_ref[row, at, :] + from_prev * preceding[h] + ratio * after[h]
                    left = jnp.where(lane == 0, lanes(west[h], -(2 * u + r)), lanes(star, 1))
                    right = jnp.where(lane == LANE - 1, lanes(east[h], -(2 * u + r) - 1), lanes(star, -1))
                    side = 2.0 * star - side_ref[row, at, :] + span_operator(star, left, right, winds[r])
                    side = fluid * side * inv
                    near = inv_near * side + near_low * subs(side, 1) + near_up * subs(side, -1)
                    out_ref[row, at, :] = inv_far * near + far_low * subs(near, 2) + far_up * subs(near, -2)
                    after = [star if n == h else after[n] for n in range(2)]
        west = [lanes(x, 8) for x in west]
        east = [lanes(x, 8) for x in east]
        return west, east, after

    lax.fori_loop(0, 16, rows, (west, east, following))


def call(kernel, out_shapes, in_specs, flops, bytes_accessed):
    return pl.pallas_call(
        kernel,
        out_shape=[jax.ShapeDtypeStruct(shape, jnp.float32) for shape in out_shapes],
        in_specs=in_specs,
        out_specs=[VMEM] * len(out_shapes),
        compiler_params=pltpu.CompilerParams(vmem_limit_bytes=LIMIT),
        cost_estimate=pl.CostEstimate(flops=flops, bytes_accessed=bytes_accessed, transcendentals=0),
    )


def on_device(concentration, courant_x, courant_y, vert_diff, emission, building):
    cells, tracers, levels, span = concentration.shape
    blocks = lax.axis_size("gx")
    devices = lax.axis_size("gy")
    c = concentration.reshape(cells, tracers * levels, span)
    cx, cy, vd, em = (
        x.reshape(cells // 2, 2 * levels, span) for x in (courant_x, courant_y, vert_diff, emission)
    )
    row = (cells, SUB, LANE)
    field = (cells, 2 * SUB, LANE)
    packed = (6, SUB, LANE)
    sent_a, sent_b = call(pack_kernel, [packed, packed], [VMEM] * 5 + [SMEM], 10**6, 2 * 10**6)(
        c, cx, cy, vd, em, building
    )
    pairs_a = [(i, i + 1) for i in range(0, devices, 2)]
    pairs_b = [(i, (i + 1) % devices) for i in range(1, devices, 2)]
    got_a = lax.ppermute(sent_a, "gy", pairs_a + [(b, a) for a, b in pairs_a])
    got_b = lax.ppermute(sent_b, "gy", pairs_b + [(b, a) for a, b in pairs_b])
    inv, prod, ends = call(factor_kernel, [row, row, (2, SUB, LANE)], [VMEM, SMEM], 10**7, 10**7)(cx, building)
    side, partial, ghost, mine = call(
        side_kernel, [field, field, (8, SUB, LANE), (7, SUB, LANE)], [VMEM] * 7 + [SMEM] + [VMEM] * 4, 10**7, 10**7
    )(c, cx, cy, vd, em, inv, ends, building, sent_a, sent_b, got_a, got_b)
    gathered = lax.all_gather(mine, "gx")
    (updated,) = call(
        functools.partial(finish_kernel, blocks), [field], [VMEM] * 8 + [SMEM], 10**7, 10**7
    )(side, partial, cy, vd, inv, prod, ghost, gathered, building)
    return updated.reshape(concentration.shape)


def solution(mesh):
    in_specs = (
        P("gx", None, None, "gy"),
        P("gx", None, "gy"),
        P("gx", None, "gy"),
        P("gx", None, "gy"),
        P("gx", None, "gy"),
        P("gx", "gy"),
    )
    return jax.shard_map(
        on_device, mesh=mesh, in_specs=in_specs, out_specs=P("gx", None, None, "gy"), check_vma=False
    )
```

profile of v0, /device:TPU:1, one launch (start us, length us, event | category | flops | bytes accessed | tf_op | source)
XLA Modules:
  0.0 51.7 jit_solution(8220114693629124311)
XLA Ops:
  0.7 0.0 copy-start
  0.7 1.2 %copy-done = f32[128,4,4,128]{3,2,1,0:T(4,128)S(1)} copy-done((f32[128,4,4,128]{3,2,1,0:T(4,128)S(1)}, f32[128,4,4,128]{3,2,1,0:T(4,128)}, u32[]{:S(2)}) %copy-start) | copy-done | bytes 1048600
  1.9 0.0 copy-start.2
  1.9 0.9 %copy-done.2 = f32[128,4,128]{2,1,0:T(4,128)S(1)} copy-done((f32[128,4,128]{2,1,0:T(4,128)S(1)}, f32[128,4,128]{2,1,0:T(4,128)}, u32[]{:S(2)}) %copy-start.2) | copy-done | bytes 262168
  2.8 0.0 copy-start.3
  2.8 0.9 %copy-done.3 = f32[128,4,128]{2,1,0:T(4,128)S(1)} copy-done((f32[128,4,128]{2,1,0:T(4,128)S(1)}, f32[128,4,128]{2,1,0:T(4,128)}, u32[]{:S(2)}) %copy-start.3) | copy-done | bytes 262168
  3.8 0.0 copy-start.5
  3.8 0.9 %copy-done.5 = f32[128,4,128]{2,1,0:T(4,128)S(1)} copy-done((f32[128,4,128]{2,1,0:T(4,128)S(1)}, f32[128,4,128]{2,1,0:T(4,128)}, u32[]{:S(2)}) %copy-start.5) | copy-done | bytes 262168
  4.7 0.0 copy-start.7
  4.7 0.9 %copy-done.7 = f32[128,4,128]{2,1,0:T(4,128)S(1)} copy-done((f32[128,4,128]{2,1,0:T(4,128)S(1)}, f32[128,4,128]{2,1,0:T(4,128)}, u32[]{:S(2)}) %copy-start.7) | copy-done | bytes 262168
  5.7 0.0 copy-start.1
  5.7 1.0 %shard_map.65 = (f32[6,8,128]{2,1,0:T(8,128)S(1)}, f32[6,8,128]{2,1,0:T(8,128)S(1)}) custom-call(f32[128,16,128]{2,1,0:T(8,128)S(1)} %bitcast.7, f32[64,8,128]{2,1,0:T(8,128)S(1)} %bitcast.9, f32[64,8,128]{2,1,0:T(8,128)S(1)} %bitcast.12, f32[64,8,128]{2,1,0:T(8,128)S(1)} %bitcast.15, f32[64,8,128]{2,1,0:T(8,128)S(1)} %bitcast.19, s32[1,1]{1,0:T(1,128)S(6)} %copy.7.building_ref), custom_call_target="tpu_custom_call" | custom-call | flops 1000000 | bytes 2000000 | tf_op jit(solution)/shard_map/pallas_call | solution.py:367
  6.6 0.0 copy-start.4
  6.7 4.1 %collective-permute-start = (f32[6,8,128]{2,1,0:T(8,128)S(1)}, f32[6,8,128]{2,1,0:T(8,128)S(1)}, u32[]{:S(2)}, u32[]{:S(2)}) collective-permute-start(f32[6,8,128]{2,1,0:T(8,128)S(1)} %get-tuple-element.16.sent_a_ref), channel_id=1, source_target_pairs={{0,1},{2,3},{4,5},{6,7},{8,9},{10,11},{12,13},{14,15},{16,17},{18,... | collective-permute-start | bytes 73736 | tf_op jit(solution)/shard_map/ppermute | solution.py:372
  10.7 12.2 %collective-permute-start.1 = (f32[6,8,128]{2,1,0:T(8,128)S(1)}, f32[6,8,128]{2,1,0:T(8,128)S(1)}, u32[]{:S(2)}, u32[]{:S(2)}) collective-permute-start(f32[6,8,128]{2,1,0:T(8,128)S(1)} %get-tuple-element.17.sent_b_ref), channel_id=1, source_target_pairs={{1,2},{3,4},{5,6},{7,8},{9,10},{11,12},{13,14},{15,16},{17,18},{19... | collective-permute-start | bytes 73736 | tf_op jit(solution)/shard_map/ppermute | solution.py:373
  22.9 1.3 %shard_map.64 = (f32[128,8,128]{2,1,0:T(8,128)S(1)}, f32[128,8,128]{2,1,0:T(8,128)S(1)}, f32[2,8,128]{2,1,0:T(8,128)S(1)}) custom-call(f32[64,8,128]{2,1,0:T(8,128)S(1)} %bitcast.10, s32[1,1]{1,0:T(1,128)S(6)} %copy.7.building_ref), custom_call_target="tpu_custom_call" | custom-call | flops 10000000 | bytes 10000000 | tf_op jit(solution)/shard_map/pallas_call | solution.py:374
  24.2 0.0 collective-permute-done.got_a_ref
  24.3 0.0 collective-permute-done.1.got_b_ref
  24.3 0.0 copy-done.1
  24.3 0.0 copy-done.4
  24.3 3.0 %shard_map.66 = (f32[128,16,128]{2,1,0:T(8,128)S(1)}, f32[128,16,128]{2,1,0:T(8,128)S(1)}, f32[8,8,128]{2,1,0:T(8,128)S(1)}, f32[7,8,128]{2,1,0:T(8,128)S(1)}) custom-call(f32[128,16,128]{2,1,0:T(8,128)S(1)} %bitcast.8, f32[64,8,128]{2,1,0:T(8,128)S(1)} %bitcast.11, f32[64,8,128]{2,1,0:T(8,128)S(1)} %bitcast.13, f32[64,8,128]{2,1,0:T(8,128)S(1)} %bitcast.16, ...), custom_call_target="tpu_custom_call" | custom-call | flops 10000000 | bytes 10000000 | tf_op jit(solution)/shard_map/pallas_call | solution.py:375
  27.3 0.0 copy-start.6
  27.4 20.5 %all-gather = f32[112,8,128]{2,1,0:T(8,128)S(1)} all-gather(f32[7,8,128]{2,1,0:T(8,128)S(1)} %get-tuple-element.22), channel_id=2, replica_groups=mesh['gx'=16,'gy'=32] {'gx'}, dimensions={0}, use_global_device_ids=true | all-gather | bytes 487424 | tf_op jit(solution)/shard_map/all_gather | solution.py:378
  47.8 0.0 copy-done.6
  47.8 3.9 %shard_map.67 = f32[128,16,128]{2,1,0:T(8,128)} custom-call(f32[128,16,128]{2,1,0:T(8,128)S(1)} %get-tuple-element.18.side_ref, f32[128,16,128]{2,1,0:T(8,128)S(1)} %get-tuple-element.19.partial_ref, f32[64,8,128]{2,1,0:T(8,128)S(1)} %bitcast.14, f32[64,8,128]{2,1,0:T(8,128)S(1)} %bitcast.17, f32[128,8,128]{2,1,0:T(8,128)S(1)} %get-tuple-element.14.inv_ref, ...), custom_call_target="tpu_custom_call" | custom-call | flops 10000000 | bytes 10000000 | tf_op jit(solution)/shard_map/pallas_call | solution.py:379
Async XLA Ops:
  0.7 1.2 %copy-start = (f32[128,4,4,128]{3,2,1,0:T(4,128)S(1)}, f32[128,4,4,128]{3,2,1,0:T(4,128)}, u32[]{:S(2)}) copy-start(f32[128,4,4,128]{3,2,1,0:T(4,128)} %param.6) | copy-start | bytes 3145732
  1.9 0.9 %copy-start.2 = (f32[128,4,128]{2,1,0:T(4,128)S(1)}, f32[128,4,128]{2,1,0:T(4,128)}, u32[]{:S(2)}) copy-start(f32[128,4,128]{2,1,0:T(4,128)} %param.7) | copy-start | bytes 786436
  2.8 0.9 %copy-start.3 = (f32[128,4,128]{2,1,0:T(4,128)S(1)}, f32[128,4,128]{2,1,0:T(4,128)}, u32[]{:S(2)}) copy-start(f32[128,4,128]{2,1,0:T(4,128)} %param.8) | copy-start | bytes 786436
  3.8 0.9 %copy-start.5 = (f32[128,4,128]{2,1,0:T(4,128)S(1)}, f32[128,4,128]{2,1,0:T(4,128)}, u32[]{:S(2)}) copy-start(f32[128,4,128]{2,1,0:T(4,128)} %param.9) | copy-start | bytes 786436
  4.7 0.9 %copy-start.7 = (f32[128,4,128]{2,1,0:T(4,128)S(1)}, f32[128,4,128]{2,1,0:T(4,128)}, u32[]{:S(2)}) copy-start(f32[128,4,128]{2,1,0:T(4,128)} %param.10) | copy-start | bytes 786436
  5.7 18.6 %copy-start.1 = (f32[128,4,4,128]{3,2,1,0:T(4,128)S(1)}, f32[128,4,4,128]{3,2,1,0:T(4,128)}, u32[]{:S(2)}) copy-start(f32[128,4,4,128]{3,2,1,0:T(4,128)} %param.6) | copy-start | bytes 3145732
  6.6 17.6 %copy-start.4 = (f32[128,4,128]{2,1,0:T(4,128)S(1)}, f32[128,4,128]{2,1,0:T(4,128)}, u32[]{:S(2)}) copy-start(f32[128,4,128]{2,1,0:T(4,128)} %param.8) | copy-start | bytes 786436
  6.7 17.6 %collective-permute-start = (f32[6,8,128]{2,1,0:T(8,128)S(1)}, f32[6,8,128]{2,1,0:T(8,128)S(1)}, u32[]{:S(2)}, u32[]{:S(2)}) collective-permute-start(f32[6,8,128]{2,1,0:T(8,128)S(1)} %get-tuple-element.16.sent_a_ref), channel_id=1, source_target_pairs={{0,1},{2,3},{4,5},{6,7},{8,9},{10,11},{12,13},{14,15},{16,17},{18,... | collective-permute-start | bytes 73736 | tf_op jit(solution)/shard_map/ppermute | solution.py:372
  10.7 13.5 %collective-permute-start.1 = (f32[6,8,128]{2,1,0:T(8,128)S(1)}, f32[6,8,128]{2,1,0:T(8,128)S(1)}, u32[]{:S(2)}, u32[]{:S(2)}) collective-permute-start(f32[6,8,128]{2,1,0:T(8,128)S(1)} %get-tuple-element.17.sent_b_ref), channel_id=1, source_target_pairs={{1,2},{3,4},{5,6},{7,8},{9,10},{11,12},{13,14},{15,16},{17,18},{19... | collective-permute-start | bytes 73736 | tf_op jit(solution)/shard_map/ppermute | solution.py:373
  27.3 20.5 %copy-start.6 = (f32[128,4,128]{2,1,0:T(4,128)S(1)}, f32[128,4,128]{2,1,0:T(4,128)}, u32[]{:S(2)}) copy-start(f32[128,4,128]{2,1,0:T(4,128)} %param.9) | copy-start | bytes 786436
where the time goes:
time: 52 us; the launch traced here: 51.7 us
  blocking collectives  20.5 us (39%)
  starting transfers between devices  16.3 us (31%)
  Pallas kernels  9.17 us (18%)
  local copies, waits for them, and re-layouts  5.03 us (10%)
  between operations  0.74 us (1%)
    all_gather x1, blocking collectives, on_device(): gathered = lax.all_gather(mine, 'gx')  20.5 us
    ppermute x1, starting transfers between devices, on_device(): got_b = lax.ppermute(sent_b, 'gy', pairs_b + [(b, a) for a, b in pairs_b])  12.2 us
    unnamed x16, local copies, waits for them, and re-layouts  5.03 us
    ppermute x1, starting transfers between devices, on_device(): got_a = lax.ppermute(sent_a, 'gy', pairs_a + [(b, a) for a, b in pairs_a])  4.07 us
    pallas_call x1, Pallas kernels, on_device(): call(functools.partial(finish_kernel, blocks), [field], [VMEM] * 8 + [SME...  3.86 us
    pallas_call x1, Pallas kernels, on_device(): call(side_kernel, [field, field, (8, SUB, LANE), (7, SUB, LANE)], [VMEM]...  3.05 us
    pallas_call x1, Pallas kernels, on_device(): call(factor_kernel, [row, row, (2, SUB, LANE)], [VMEM, SMEM], 10 ** 7, 10...  1.29 us
  transfers between devices with their start and end apart: 2, of which 0 were waited for; matrix products, arithmetic and copies ran while one was open for 0% of the time, Pallas kernels for 2%

commit v1 on v0

v1 whole, which is shorter than its diff:
```python
import functools

import jax
import jax.numpy as jnp
from jax import lax
from jax.experimental import pallas as pl
from jax.experimental.pallas import tpu as pltpu
from jax.sharding import PartitionSpec as P

cross_diff = 300.0
span_diff = 0.25

SUB, LANE = 8, 128
VMEM = pl.BlockSpec(memory_space=pltpu.VMEM)
HBM = pl.BlockSpec(memory_space=pltpu.HBM)
SMEM = pl.BlockSpec(memory_space=pltpu.SMEM)
LIMIT = 16 * 1024 * 1024
(INV, PULLED, FROM_PREV, WEST, EAST, CENTRE, BELOW, ABOVE, NEAR, NEAR_LOW, NEAR_UP, FAR, FAR_LOW, FAR_UP) = range(14)
KEPT = 14
CHUNKS = 4


def sub_ids():
    return lax.broadcasted_iota(jnp.int32, (SUB, LANE), 0)


def lane_ids():
    return lax.broadcasted_iota(jnp.int32, (SUB, LANE), 1)


def lanes(x, shift):
    shift %= LANE
    return pltpu.roll(x, shift, 1) if shift else x


def subs(x, shift):
    shift %= SUB
    return pltpu.roll(x, shift, 0) if shift else x


def fluid_of(building_ref):
    return 1.0 - building_ref[0, 0].astype(jnp.float32)


def both_rows(pair):
    low = sub_ids() < 4
    turned = subs(pair, 4)
    return jnp.where(low, pair, turned), jnp.where(low, turned, pair)


def level_above(x):
    return jnp.where(sub_ids() % 4 == 3, 0.0, subs(x, -1))


def level_below(x):
    return jnp.where(sub_ids() % 4 == 0, 0.0, subs(x, 1))


def edge_quads(west, east):
    at_west = lane_ids() % 4 == 2
    return [jnp.where(at_west, lanes(west, 2 - g), lanes(east, 1 - g)) for g in range(4)]


def neighbours(q, quads, row):
    base, offset = row
    edge = pltpu.roll(quads[offset % 4], 126 - base - offset // 4 * 4, 1)
    lane = lane_ids()
    return jnp.where(lane == 0, edge, lanes(q, 1)), jnp.where(lane == LANE - 1, edge, lanes(q, -1))


def pack_kernel(
    c_hbm, cx_hbm, cy_hbm, vd_hbm, em_hbm, building_ref,
    a_ref, b_ref, c_ref, cx_ref, cy_ref, vd_ref, em_ref, sems,
):
    coefs = ((cx_hbm, cx_ref), (cy_hbm, cy_ref), (vd_hbm, vd_ref), (em_hbm, em_ref))
    size = c_ref.shape[0] // CHUNKS
    copies = [
        pltpu.make_async_copy(c_hbm.at[pl.ds(n * size, size)], c_ref.at[pl.ds(n * size, size)], sems.at[n])
        for n in range(CHUNKS)
    ]
    copies += [pltpu.make_async_copy(src, dst, sems.at[CHUNKS + n]) for n, (src, dst) in enumerate(coefs)]
    for copy in copies:
        copy.start()

    lane, sub = lane_ids(), sub_ids()
    fluid = fluid_of(building_ref)
    low = sub < 4
    even_gy = lax.rem(lax.axis_index("gy"), 2) == 0
    quarter = lane // 4
    zero = jnp.zeros((SUB, LANE), jnp.float32)
    picked = [[zero] * 4 for _ in range(2)]
    for n in range(CHUNKS):
        copies[n].wait()
        for m in range(n * size // 4, (n + 1) * size // 4):
            here = quarter == m
            for g in range(4):
                for half in range(2):
                    turned = lanes(c_ref[4 * m + g, 8 * half : 8 * half + 8, :], 4 * m + 2)
                    picked[half][g] = jnp.where(here, turned, picked[half][g])
    columns = []
    for half in range(2):
        found = []
        for j in range(4):
            out = lanes(picked[half][0], -j)
            for g in range(1, 4):
                out = jnp.where(lane % 4 == g, lanes(picked[half][g], g - j), out)
            found.append(out)
        columns.append(found)
    even = lane % 2 == 0
    pair_of = lane // 2
    first, last = [], []
    for n, (_, ref) in enumerate(coefs):
        copies[CHUNKS + n].wait()
        acc = zero
        for k in range(64):
            acc = jnp.where(pair_of == k, lanes(ref[k], 2 * k + 1), acc)
        turned = subs(acc, 4)
        at_even = jnp.where(low, acc, turned)
        at_odd = jnp.where(low, turned, acc)
        last.append(jnp.where(even, at_even, lanes(at_odd, 1)))
        first.append(jnp.where(even, lanes(at_even, -1), at_odd))
    sides = []
    for (outer, inner), edge in (((2, 3), first), ((1, 0), last)):
        pull = fluid * (edge[0] + cross_diff)
        sides.append(
            [
                columns[0][outer],
                columns[1][outer],
                columns[0][inner],
                columns[1][inner],
                jnp.where(low, pull, edge[1]),
                jnp.where(low, edge[2], edge[3]),
            ]
        )
    for n in range(6):
        to_left, to_right = sides[0][n], sides[1][n]
        a_ref[n] = jnp.where(even_gy, to_right, to_left)
        b_ref[n] = jnp.where(even_gy, to_left, to_right)


def factor_kernel(cx_ref, cy_ref, vd_ref, building_ref, kept_ref, ends_ref):
    fluid = fluid_of(building_ref)
    push = cross_diff * fluid
    ground = sub_ids() % 4 == 0

    def rows(k, state):
        ratio, from_prev, chain, first_prev = state
        for u in range(4):
            pair = 4 * k + u
            wind, face = cy_ref[pair], vd_ref[pair]
            face_up = level_above(face)
            west = fluid * (jnp.maximum(wind, 0.0) + span_diff)
            east = fluid * (jnp.maximum(-wind, 0.0) + span_diff)
            inv = 1.0 / (1.0 + face + face_up)
            lower = jnp.where(ground, 0.0, face * inv)
            upper = face_up * inv
            near = 1.0 / (1.0 - lower * subs(upper, 1) - upper * subs(lower, -1))
            near_low, near_up = near * lower, near * upper
            far_low, far_up = near_low * subs(lower, 1), near_up * subs(upper, -1)
            far = 1.0 / (1.0 - far_low * subs(far_up, 2) - far_up * subs(far_low, -2))
            scale = fluid * inv
            pairs = {
                WEST: west,
                EAST: east,
                CENTRE: fluid * (1.0 - face - face_up) - west - east,
                BELOW: jnp.where(ground, 0.0, fluid * face),
                ABOVE: fluid * face_up,
                NEAR: near * scale,
                NEAR_LOW: near_low * subs(scale, 1),
                NEAR_UP: near_up * subs(scale, -1),
                FAR: far,
                FAR_LOW: far * far_low,
                FAR_UP: far * far_up,
            }
            for n, value in pairs.items():
                kept_ref[2 * pair, n], kept_ref[2 * pair + 1, n] = both_rows(value)
            for r, pull in enumerate(both_rows(fluid * (cx_ref[pair] + cross_diff))):
                row = 2 * pair + r
                inv = 1.0 / ((1.0 + pull + push) - pull * ratio)
                pulled = pull * inv
                from_prev = pulled * from_prev
                first_prev = first_prev + chain * from_prev
                ratio = push * inv
                chain = chain * ratio
                kept_ref[row, INV] = inv
                kept_ref[row, PULLED] = pulled
                kept_ref[row, FROM_PREV] = from_prev
        return ratio, from_prev, chain, first_prev

    zero = jnp.zeros((SUB, LANE), jnp.float32)
    ratio, from_prev, chain, first_prev = lax.fori_loop(0, 16, rows, (zero, zero + 1.0, zero + 1.0, zero))
    low = sub_ids() < 4
    ends_ref[0] = jnp.where(low, first_prev, chain)
    ends_ref[1] = jnp.where(low, from_prev, ratio)


def merge(left, right, part):
    low = sub_ids() < 4
    return jnp.where(low, left, subs(right, 4)) if part == 0 else jnp.where(low, subs(left, 4), right)


def ghost_columns(from_left, from_right, own_left, own_right):
    lane, sub = lane_ids(), sub_ids()
    pull, wind = merge(from_left[4], from_right[4], 0), merge(from_left[4], from_right[4], 1)
    face, emitted = merge(from_left[5], from_right[5], 0), merge(from_left[5], from_right[5], 1)
    fluid = jnp.where(pull > 0.0, 1.0, 0.0)
    face_up = level_above(face)
    west = jnp.maximum(wind, 0.0) + span_diff
    east = jnp.maximum(-wind, 0.0) + span_diff
    inv = 1.0 / (1.0 + pull + cross_diff * fluid)
    lower = pull * inv
    upper = cross_diff * fluid * inv
    sides = []
    for t in range(4):
        h, part = t // 2, t % 2
        q = merge(from_left[h], from_right[h], part)
        left = merge(from_left[2 + h], own_right[h], part)
        right = merge(own_left[h], from_right[2 + h], part)
        side = q + west * (left - q) + east * (right - q)
        side = side + face * (level_below(q) - q) + face_up * (level_above(q) - q)
        side = side + jnp.where(sub % 4 == 0, subs(emitted, -t), 0.0)
        sides.append(inv * fluid * side)
    sides.append(jnp.where(lane == 0, lower, 0.0))
    sides.append(jnp.where(lane == LANE - 1, upper, 0.0))
    lower = jnp.where(lane == 0, 0.0, lower)
    upper = jnp.where(lane == LANE - 1, 0.0, upper)
    step = 1
    while step < LANE:
        low_prev, up_prev = lanes(lower, step), lanes(upper, step)
        low_next, up_next = lanes(lower, -step), lanes(upper, -step)
        inv = 1.0 / (1.0 - lower * up_prev - upper * low_next)
        from_low, from_up = inv * lower, inv * upper
        sides = [inv * s + from_low * lanes(s, step) + from_up * lanes(s, -step) for s in sides]
        lower, upper = from_low * low_prev, from_up * up_next
        step *= 2
    prev, following = both_rows(sides[4]), both_rows(sides[5])
    return [
        [merge(sides[0], sides[1], s), merge(sides[2], sides[3], s), prev[s], following[s]] for s in range(2)
    ]


def side_kernel(
    c_ref, em_ref, kept_ref, ends_ref, building_ref, sent_a_ref, sent_b_ref, got_a_ref, got_b_ref,
    side_ref, partial_ref, ghost_ref, rows_ref,
):
    lane, sub = lane_ids(), sub_ids()
    fluid = fluid_of(building_ref)
    push = cross_diff * fluid
    even_gy = lax.rem(lax.axis_index("gy"), 2) == 0
    own_left = [jnp.where(even_gy, sent_b_ref[n], sent_a_ref[n]) for n in range(2)]
    own_right = [jnp.where(even_gy, sent_a_ref[n], sent_b_ref[n]) for n in range(2)]
    from_left = [jnp.where(even_gy, got_b_ref[n], got_a_ref[n]) for n in range(6)]
    from_right = [jnp.where(even_gy, got_a_ref[n], got_b_ref[n]) for n in range(6)]

    extra = jnp.zeros((SUB, LANE), jnp.float32)
    for s, parts in enumerate(ghost_columns(from_left, from_right, own_left, own_right)):
        for n in range(4):
            ghost_ref[4 * s + n] = parts[n]
        ends = [
            (parts[0], 0), (parts[1], 0), (parts[0], 1), (parts[1], 1),
            (parts[2], 0), (parts[3], 0), (parts[2], 1), (parts[3], 1),
        ]
        for j, (part, tail) in enumerate(ends):
            extra = jnp.where(lane == 2 * j + s, lanes(part, 2 * j + s + tail), extra)

    quads = [edge_quads(from_left[h], from_right[h]) for h in range(2)]

    def rows(k, state):
        last, first, chain = state
        for n in range(8):
            row, pair = 8 * k + n, 4 * k + n // 2
            inv, pulled = kept_ref[row, INV], kept_ref[row, PULLED]
            west, east, centre = kept_ref[row, WEST], kept_ref[row, EAST], kept_ref[row, CENTRE]
            below, above = kept_ref[row, BELOW], kept_ref[row, ABOVE]
            new_last, new_first = [], []
            for h in range(2):
                q = c_ref[row, 8 * h : 8 * h + 8, :]
                left, right = neighbours(q, quads[h], (8 * k, n))
                tracer = 4 * (n % 2) + 2 * h
                source = jnp.where(
                    sub == 0,
                    em_ref[pair, tracer : tracer + 1, :],
                    jnp.where(sub == 4, em_ref[pair, tracer + 1 : tracer + 2, :], 0.0),
                )
                side = (centre * q + fluid * source) + (west * left + east * right)
                side = side + (below * subs(q, 1) + above * subs(q, -1))
                value = side * inv + pulled * last[h]
                side_ref[row, 8 * h : 8 * h + 8, :] = side
                partial_ref[row, 8 * h : 8 * h + 8, :] = value
                new_last.append(value)
                new_first.append(first[h] + chain * value)
            last, first = new_last, new_first
            chain = chain * (push * inv)
        return last, first, chain

    zero = jnp.zeros((SUB, LANE), jnp.float32)
    last, first, _ = lax.fori_loop(0, 16, rows, ([zero, zero], [zero, zero], zero + 1.0))
    rows_ref[0], rows_ref[1] = first
    rows_ref[2], rows_ref[3] = last
    rows_ref[4] = ends_ref[0]
    rows_ref[5] = ends_ref[1]
    rows_ref[6] = extra


def interface(blocks, place):
    zero = jnp.zeros((SUB, LANE), jnp.float32)
    own, slope = [zero, zero], zero
    kept_own, kept_slope = own, slope
    forms = []
    for k, (first, last, first_prev, first_next, last_prev, last_next) in enumerate(blocks):
        here = place == k
        kept_own = [jnp.where(here, own[h], kept_own[h]) for h in range(2)]
        kept_slope = jnp.where(here, slope, kept_slope)
        inv = 1.0 / (1.0 - first_prev * slope)
        start = [(first[h] + first_prev * own[h]) * inv for h in range(2)]
        start_next = first_next * inv
        forms.append((start, start_next))
        carried = last_prev * slope
        own = [last[h] + last_prev * own[h] + carried * start[h] for h in range(2)]
        slope = last_next + carried * start_next
    after = [zero, zero]
    following, mine = after, after
    for k in reversed(range(len(forms))):
        following = [jnp.where(place == k, after[h], following[h]) for h in range(2)]
        start, start_next = forms[k]
        after = [start[h] + start_next * after[h] for h in range(2)]
        mine = [jnp.where(place == k, after[h], mine[h]) for h in range(2)]
    preceding = [kept_own[h] + kept_slope * mine[h] for h in range(2)]
    return preceding, following


def finish_kernel(blocks, side_ref, partial_ref, kept_ref, ghost_ref, rows_ref, building_ref, out_ref):
    push = cross_diff * fluid_of(building_ref)
    place = lax.axis_index("gx")
    main, extra = [], []
    for k in range(blocks):
        first_prev, first_next = both_rows(rows_ref[k, 4])
        last_prev, last_next = both_rows(rows_ref[k, 5])
        main.append(
            ([rows_ref[k, 0], rows_ref[k, 1]], [rows_ref[k, 2], rows_ref[k, 3]],
             first_prev, first_next, last_prev, last_next)
        )
        e = [lanes(rows_ref[k, 6], -2 * j) for j in range(8)]
        extra.append((e[0:2], e[2:4], e[4], e[5], e[6], e[7]))
    preceding, following = interface(main, place)
    ghost_prev, ghost_next = interface(extra, place)
    ghosts = []
    for s in range(2):
        ghosts.append(
            [
                ghost_ref[4 * s + h]
                + ghost_ref[4 * s + 2] * ghost_prev[h][:, s : s + 1]
                + ghost_ref[4 * s + 3] * ghost_next[h][:, s : s + 1]
                for h in range(2)
            ]
        )
    quads = [edge_quads(ghosts[0][h], ghosts[1][h]) for h in range(2)]

    def rows(step, after):
        k = 15 - step
        for n in reversed(range(8)):
            row = 8 * k + n
            ratio, from_prev = push * kept_ref[row, INV], kept_ref[row, FROM_PREV]
            west, east = kept_ref[row, WEST], kept_ref[row, EAST]
            near, near_low, near_up = kept_ref[row, NEAR], kept_ref[row, NEAR_LOW], kept_ref[row, NEAR_UP]
            far, far_low, far_up = kept_ref[row, FAR], kept_ref[row, FAR_LOW], kept_ref[row, FAR_UP]
            centre = 2.0 - west - east
            new_after = []
            for h in range(2):
                at = slice(8 * h, 8 * h + 8)
                star = (partial_ref[row, at, :] + from_prev * preceding[h]) + ratio * after[h]
                left, right = neighbours(star, quads[h], (8 * k, n))
                side = (centre * star - side_ref[row, at, :]) + (west * left + east * right)
                value = near * side + near_low * subs(side, 1) + near_up * subs(side, -1)
                out_ref[row, at, :] = far * value + far_low * subs(value, 2) + far_up * subs(value, -2)
                new_after.append(star)
            after = new_after
        return after

    lax.fori_loop(0, 16, rows, following)


def call(kernel, out_shapes, in_specs, flops, bytes_accessed, limit=LIMIT, scratch=()):
    return pl.pallas_call(
        kernel,
        out_shape=[jax.ShapeDtypeStruct(shape, jnp.float32) for shape in out_shapes],
        in_specs=in_specs,
        out_specs=[VMEM] * len(out_shapes),
        scratch_shapes=list(scratch),
        compiler_params=pltpu.CompilerParams(vmem_limit_bytes=limit),
        cost_estimate=pl.CostEstimate(flops=flops, bytes_accessed=bytes_accessed, transcendentals=0),
    )


def on_device(concentration, courant_x, courant_y, vert_diff, emission, building):
    cells, tracers, levels, span = concentration.shape
    blocks = lax.axis_size("gx")
    devices = lax.axis_size("gy")
    c = concentration.reshape(cells, tracers * levels, span)
    coefs = [x.reshape(cells // 2, 2 * levels, span) for x in (courant_x, courant_y, vert_diff, emission)]
    field = (cells, 2 * SUB, LANE)
    packed = (6, SUB, LANE)
    sent_a, sent_b, c, cx, cy, vd, em = call(
        pack_kernel,
        [packed, packed, field] + [x.shape for x in coefs],
        [HBM] * 5 + [SMEM],
        10**6,
        2 * 10**6,
        scratch=[pltpu.SemaphoreType.DMA((CHUNKS + 4,))],
    )(*(pltpu.with_memory_space_constraint(x, pltpu.HBM) for x in (c, *coefs)), building)
    pairs_a = [(i, i + 1) for i in range(0, devices, 2)]
    pairs_b = [(i, (i + 1) % devices) for i in range(1, devices, 2)]
    got_a = lax.ppermute(sent_a, "gy", pairs_a + [(b, a) for a, b in pairs_a])
    got_b = lax.ppermute(sent_b, "gy", pairs_b + [(b, a) for a, b in pairs_b])
    kept, ends = call(
        factor_kernel, [(cells, KEPT, SUB, LANE), (2, SUB, LANE)], [VMEM] * 3 + [SMEM], 10**7, 10**7
    )(cx, cy, vd, building)
    side, partial, ghost, mine = call(
        side_kernel, [field, field, (8, SUB, LANE), (7, SUB, LANE)], [VMEM] * 4 + [SMEM] + [VMEM] * 4, 10**7, 10**7
    )(c, em, kept, ends, building, sent_a, sent_b, got_a, got_b)
    gathered = lax.all_gather(mine, "gx")
    (updated,) = call(functools.partial(finish_kernel, blocks), [field], [VMEM] * 5 + [SMEM], 10**7, 10**7)(
        side, partial, kept, ghost, gathered, building
    )
    return updated.reshape(concentration.shape)


def solution(mesh):
    in_specs = (
        P("gx", None, None, "gy"),
        P("gx", None, "gy"),
        P("gx", None, "gy"),
        P("gx", None, "gy"),
        P("gx", None, "gy"),
        P("gx", "gy"),
    )
    return jax.shard_map(
        on_device, mesh=mesh, in_specs=in_specs, out_specs=P("gx", None, None, "gy"), check_vma=False
    )
```

time: 52 us -> 47.5 us (0.913)
  local copies, waits for them, and re-layouts: 5.03 us -> 0 us
  Pallas kernels: 9.17 us -> 10.1 us
    unnamed x16 -> x0, local copies, waits for them, and re-layouts: 5.03 us -> none
    pallas_call x3, Pallas kernels: 6.12 us -> 7.34 us  [the longest x1 3.53 us: on_device(): call(functools.partial(finish_kernel, blocks), [field], [VMEM] * 5 + [SME...]
  transfers between devices with their start and end apart: 2 -> 2, of which waited for: 0 -> 0; matrix products, arithmetic and copies ran while one was open for 0% -> 0% of each run, Pallas kernels for 2% -> 3%
where the time goes in v1:
time: 47.5 us; the launch traced here: 47.3 us
  blocking collectives  20.3 us (43%)
  starting transfers between devices  16.1 us (34%)
  Pallas kernels  10.1 us (21%)
  between operations  0.71 us (1%)
    all_gather x1, blocking collectives, on_device(): gathered = lax.all_gather(mine, 'gx')  20.3 us
    ppermute x1, starting transfers between devices, on_device(): got_b = lax.ppermute(sent_b, 'gy', pairs_b + [(b, a) for a, b in pairs_b])  12.2 us
    ppermute x1, starting transfers between devices, on_device(): got_a = lax.ppermute(sent_a, 'gy', pairs_a + [(b, a) for a, b in pairs_a])  3.95 us
    pallas_call x1, Pallas kernels, on_device(): call(functools.partial(finish_kernel, blocks), [field], [VMEM] * 5 + [SME...  3.53 us
    pallas_call x1, Pallas kernels, on_device(): call(side_kernel, [field, field, (8, SUB, LANE), (7, SUB, LANE)], [VMEM]...  2.78 us
    pallas_call x1, Pallas kernels, on_device(): call(pack_kernel, [packed, packed, field] + [x.shape for x in coefs], [HB...  2.47 us
    pallas_call x1, Pallas kernels, on_device(): call(factor_kernel, [(cells, KEPT, SUB, LANE), (2, SUB, LANE)], [VMEM] *...  1.34 us
  transfers between devices with their start and end apart: 2, of which 0 were waited for; matrix products, arithmetic and copies ran while one was open for 0% of the time, Pallas kernels for 3%

profile of v1, /device:TPU:1, one launch (start us, length us, event | category | flops | bytes accessed | tf_op | source)
XLA Modules:
  0.0 47.3 jit_solution(4896336166735697076)
XLA Ops:
  0.7 2.5 %shard_map.64 = (f32[6,8,128]{2,1,0:T(8,128)S(1)}, f32[6,8,128]{2,1,0:T(8,128)S(1)}, f32[128,16,128]{2,1,0:T(8,128)S(1)}, f32[64,8,128]{2,1,0:T(8,128)S(1)}, f32...) custom-call(f32[128,16,128]{2,1,0:T(8,128)} %bitcast.8, f32[64,8,128]{2,1,0:T(8,128)} %bitcast.9, ...), custom_call_target="tpu_custom_call" | custom-call | flops 1000000 | bytes 2000000 | tf_op jit(solution)/shard_map/pallas_call | solution.py:403
  3.1 3.9 %collective-permute-start = (f32[6,8,128]{2,1,0:T(8,128)S(1)}, f32[6,8,128]{2,1,0:T(8,128)S(1)}, u32[]{:S(2)}, u32[]{:S(2)}) collective-permute-start(f32[6,8,128]{2,1,0:T(8,128)S(1)} %get-tuple-element.25.sent_a_ref), channel_id=1, source_target_pairs={{0,1},{2,3},{4,5},{6,7},{8,9},{10,11},{12,13},{14,15},{16,17},{18,... | collective-permute-start | bytes 73736 | tf_op jit(solution)/shard_map/ppermute | solution.py:413
  7.1 12.2 %collective-permute-start.1 = (f32[6,8,128]{2,1,0:T(8,128)S(1)}, f32[6,8,128]{2,1,0:T(8,128)S(1)}, u32[]{:S(2)}, u32[]{:S(2)}) collective-permute-start(f32[6,8,128]{2,1,0:T(8,128)S(1)} %get-tuple-element.26.sent_b_ref), channel_id=1, source_target_pairs={{1,2},{3,4},{5,6},{7,8},{9,10},{11,12},{13,14},{15,16},{17,18},{19... | collective-permute-start | bytes 73736 | tf_op jit(solution)/shard_map/ppermute | solution.py:414
  19.3 1.3 %shard_map.65 = (f32[128,14,8,128]{3,2,1,0:T(8,128)S(1)}, f32[2,8,128]{2,1,0:T(8,128)S(1)}) custom-call(f32[64,8,128]{2,1,0:T(8,128)S(1)} %get-tuple-element.20.cx_ref, f32[64,8,128]{2,1,0:T(8,128)S(1)} %get-tuple-element.21.cy_ref, f32[64,8,128]{2,1,0:T(8,128)S(1)} %get-tuple-element.22.vd_ref, s32[1,1]{1,0:T(1,128)S(6)} %copy.7.building_ref), custom_call_target="tpu_custom_call" | custom-call | flops 10000000 | bytes 10000000 | tf_op jit(solution)/shard_map/pallas_call | solution.py:415
  20.6 0.0 collective-permute-done.got_a_ref
  20.7 0.0 collective-permute-done.1.got_b_ref
  20.7 2.8 %shard_map.66 = (f32[128,16,128]{2,1,0:T(8,128)S(1)}, f32[128,16,128]{2,1,0:T(8,128)S(1)}, f32[8,8,128]{2,1,0:T(8,128)S(1)}, f32[7,8,128]{2,1,0:T(8,128)S(1)}) custom-call(f32[128,16,128]{2,1,0:T(8,128)S(1)} %get-tuple-element.18.c_ref, f32[64,8,128]{2,1,0:T(8,128)S(1)} %get-tuple-element.19.em_ref, f32[128,14,8,128]{3,2,1,0:T(8,128)S(1)} %get-tuple-element.23.kept_ref, ...), custom_call_target="tpu_custom_call" | custom-call | flops 10000000 | bytes 10000000 | tf_op jit(solution)/shard_map/pallas_call | solution.py:418
  23.5 20.3 %all-gather = f32[112,8,128]{2,1,0:T(8,128)S(1)} all-gather(f32[7,8,128]{2,1,0:T(8,128)S(1)} %get-tuple-element.30), channel_id=2, replica_groups=mesh['gx'=16,'gy'=32] {'gx'}, dimensions={0}, use_global_device_ids=true | all-gather | bytes 487424 | tf_op jit(solution)/shard_map/all_gather | solution.py:421
  43.8 3.5 %shard_map.67 = f32[128,16,128]{2,1,0:T(8,128)} custom-call(f32[128,16,128]{2,1,0:T(8,128)S(1)} %get-tuple-element.27.side_ref, f32[128,16,128]{2,1,0:T(8,128)S(1)} %get-tuple-element.28.partial_ref, f32[128,14,8,128]{3,2,1,0:T(8,128)S(1)} %get-tuple-element.23.kept_ref, f32[8,8,128]{2,1,0:T(8,128)S(1)} %get-tuple-element.29.ghost_ref, ...), custom_call_target="tpu_custom_call" | custom-call | flops 10000000 | bytes 10000000 | tf_op jit(solution)/shard_map/pallas_call | solution.py:422
Async XLA Ops:
  3.1 17.5 %collective-permute-start = (f32[6,8,128]{2,1,0:T(8,128)S(1)}, f32[6,8,128]{2,1,0:T(8,128)S(1)}, u32[]{:S(2)}, u32[]{:S(2)}) collective-permute-start(f32[6,8,128]{2,1,0:T(8,128)S(1)} %get-tuple-element.25.sent_a_ref), channel_id=1, source_target_pairs={{0,1},{2,3},{4,5},{6,7},{8,9},{10,11},{12,13},{14,15},{16,17},{18,... | collective-permute-start | bytes 73736 | tf_op jit(solution)/shard_map/ppermute | solution.py:413
  7.1 13.6 %collective-permute-start.1 = (f32[6,8,128]{2,1,0:T(8,128)S(1)}, f32[6,8,128]{2,1,0:T(8,128)S(1)}, u32[]{:S(2)}, u32[]{:S(2)}) collective-permute-start(f32[6,8,128]{2,1,0:T(8,128)S(1)} %get-tuple-element.26.sent_b_ref), channel_id=1, source_target_pairs={{1,2},{3,4},{5,6},{7,8},{9,10},{11,12},{13,14},{15,16},{17,18},{19... | collective-permute-start | bytes 73736 | tf_op jit(solution)/shard_map/ppermute | solution.py:414

commit v2 on v1

--- a/solution.py
+++ b/solution.py
@@ -240,7 +240,7 @@
 
 
 def side_kernel(
-    c_ref, em_ref, kept_ref, ends_ref, building_ref, sent_a_ref, sent_b_ref, got_a_ref, got_b_ref,
+    c_ref, em_ref, kept_ref, ends_ref, building_ref, sent_b_ref, sent_a_ref, got_b_ref, got_a_ref,
     side_ref, partial_ref, ghost_ref, rows_ref,
 ):
     lane, sub = lane_ids(), sub_ids()
@@ -302,15 +302,61 @@
     rows_ref[6] = extra
 
 
-def interface(blocks, place):
+def blocks_of(rows_ref):
+    main, extra = [], []
+    for k in range(rows_ref.shape[0]):
+        first_prev, first_next = both_rows(rows_ref[k, 4])
+        last_prev, last_next = both_rows(rows_ref[k, 5])
+        main.append(
+            ([rows_ref[k, 0], rows_ref[k, 1]], [rows_ref[k, 2], rows_ref[k, 3]],
+             first_prev, first_next, last_prev, last_next)
+        )
+        e = [lanes(rows_ref[k, 6], -2 * j) for j in range(8)]
+        extra.append((e[0:2], e[2:4], e[4], e[5], e[6], e[7]))
+    return main, extra
+
+
+def joined(before, after):
+    first, last, first_prev, first_next, last_prev, last_next = before
+    first_b, last_b, first_prev_b, first_next_b, last_prev_b, last_next_b = after
+    inv = 1.0 / (1.0 - last_next * first_prev_b)
+    low_own = [(last[h] + last_next * first_b[h]) * inv for h in range(2)]
+    low_prev, low_next = last_prev * inv, last_next * first_next_b * inv
+    high_own = [first_b[h] + first_prev_b * low_own[h] for h in range(2)]
+    high_prev, high_next = first_prev_b * low_prev, first_next_b + first_prev_b * low_next
+    return (
+        [first[h] + first_next * high_own[h] for h in range(2)],
+        [last_b[h] + last_prev_b * low_own[h] for h in range(2)],
+        first_prev + first_next * high_prev,
+        first_next * high_next,
+        last_prev_b * low_prev,
+        last_next_b + last_prev_b * low_next,
+    )
+
+
+def condense_kernel(rows_ref, out_ref):
+    main, extra = (functools.reduce(joined, forms) for forms in blocks_of(rows_ref))
+    low, lane = sub_ids() < 4, lane_ids()
+    out_ref[0], out_ref[1] = main[0]
+    out_ref[2], out_ref[3] = main[1]
+    out_ref[4] = jnp.where(low, main[2], main[3])
+    out_ref[5] = jnp.where(low, main[4], main[5])
+    packed = extra[0][0]
+    for j, part in enumerate((extra[0][1], *extra[1], *extra[2:]), 1):
+        packed = jnp.where(lane // 2 == j, lanes(part, 2 * j), packed)
+    out_ref[6] = packed
+
+
+def interface(blocks, place, before, beyond):
     zero = jnp.zeros((SUB, LANE), jnp.float32)
-    own, slope = [zero, zero], zero
+    own, slope = before, zero
     kept_own, kept_slope = own, slope
     forms = []
     for k, (first, last, first_prev, first_next, last_prev, last_next) in enumerate(blocks):
-        here = place == k
-        kept_own = [jnp.where(here, own[h], kept_own[h]) for h in range(2)]
-        kept_slope = jnp.where(here, slope, kept_slope)
+        if k:
+            here = place == k
+            kept_own = [jnp.where(here, own[h], kept_own[h]) for h in range(2)]
+            kept_slope = jnp.where(here, slope, kept_slope)
         inv = 1.0 / (1.0 - first_prev * slope)
         start = [(first[h] + first_prev * own[h]) * inv for h in range(2)]
         start_next = first_next * inv
@@ -318,7 +364,7 @@
         carried = last_prev * slope
         own = [last[h] + last_prev * own[h] + carried * start[h] for h in range(2)]
         slope = last_next + carried * start_next
-    after = [zero, zero]
+    after = beyond
     following, mine = after, after
     for k in reversed(range(len(forms))):
         following = [jnp.where(place == k, after[h], following[h]) for h in range(2)]
@@ -329,21 +375,21 @@
     return preceding, following
 
 
-def finish_kernel(blocks, side_ref, partial_ref, kept_ref, ghost_ref, rows_ref, building_ref, out_ref):
+def finish_kernel(
+    side_ref, partial_ref, kept_ref, ghost_ref, near_ref, pair_ref, half_ref, building_ref, out_hbm, out_ref, sems
+):
     push = cross_diff * fluid_of(building_ref)
     place = lax.axis_index("gx")
-    main, extra = [], []
-    for k in range(blocks):
-        first_prev, first_next = both_rows(rows_ref[k, 4])
-        last_prev, last_next = both_rows(rows_ref[k, 5])
-        main.append(
-            ([rows_ref[k, 0], rows_ref[k, 1]], [rows_ref[k, 2], rows_ref[k, 3]],
-             first_prev, first_next, last_prev, last_next)
-        )
-        e = [lanes(rows_ref[k, 6], -2 * j) for j in range(8)]
-        extra.append((e[0:2], e[2:4], e[4], e[5], e[6], e[7]))
-    preceding, following = interface(main, place)
-    ghost_prev, ghost_next = interface(extra, place)
+    quarter = near_ref.shape[0]
+    zero = jnp.zeros((SUB, LANE), jnp.float32)
+    preceding, following = [zero, zero], [zero, zero]
+    ghost_prev, ghost_next = preceding, following
+    for ref, at in (
+        (half_ref, place // (2 * quarter)), (pair_ref, place // quarter % 2), (near_ref, place % quarter)
+    ):
+        main, extra = blocks_of(ref)
+        preceding, following = interface(main, at, preceding, following)
+        ghost_prev, ghost_next = interface(extra, at, ghost_prev, ghost_next)
     ghosts = []
     for s in range(2):
         ghosts.append(
@@ -375,17 +421,23 @@
                 out_ref[row, at, :] = far * value + far_low * subs(value, 2) + far_up * subs(value, -2)
                 new_after.append(star)
             after = new_after
+        written(k).start()
         return after
 
+    def written(k):
+        return pltpu.make_async_copy(out_ref.at[pl.ds(8 * k, 8)], out_hbm.at[pl.ds(8 * k, 8)], sems.at[k])
+
     lax.fori_loop(0, 16, rows, following)
-
-
-def call(kernel, out_shapes, in_specs, flops, bytes_accessed, limit=LIMIT, scratch=()):
+    for k in range(16):
+        written(k).wait()
+
+
+def call(kernel, out_shapes, in_specs, flops, bytes_accessed, limit=LIMIT, scratch=(), out_space=VMEM):
     return pl.pallas_call(
         kernel,
         out_shape=[jax.ShapeDtypeStruct(shape, jnp.float32) for shape in out_shapes],
         in_specs=in_specs,
-        out_specs=[VMEM] * len(out_shapes),
+        out_specs=[out_space] * len(out_shapes),
         scratch_shapes=list(scratch),
         compiler_params=pltpu.CompilerParams(vmem_limit_bytes=limit),
         cost_estimate=pl.CostEstimate(flops=flops, bytes_accessed=bytes_accessed, transcendentals=0),
@@ -410,18 +462,32 @@
     )(*(pltpu.with_memory_space_constraint(x, pltpu.HBM) for x in (c, *coefs)), building)
     pairs_a = [(i, i + 1) for i in range(0, devices, 2)]
     pairs_b = [(i, (i + 1) % devices) for i in range(1, devices, 2)]
+    got_b = lax.ppermute(sent_b, "gy", pairs_b + [(b, a) for a, b in pairs_b])
     got_a = lax.ppermute(sent_a, "gy", pairs_a + [(b, a) for a, b in pairs_a])
-    got_b = lax.ppermute(sent_b, "gy", pairs_b + [(b, a) for a, b in pairs_b])
     kept, ends = call(
         factor_kernel, [(cells, KEPT, SUB, LANE), (2, SUB, LANE)], [VMEM] * 3 + [SMEM], 10**7, 10**7
     )(cx, cy, vd, building)
     side, partial, ghost, mine = call(
         side_kernel, [field, field, (8, SUB, LANE), (7, SUB, LANE)], [VMEM] * 4 + [SMEM] + [VMEM] * 4, 10**7, 10**7
-    )(c, em, kept, ends, building, sent_a, sent_b, got_a, got_b)
-    gathered = lax.all_gather(mine, "gx")
-    (updated,) = call(functools.partial(finish_kernel, blocks), [field], [VMEM] * 5 + [SMEM], 10**7, 10**7)(
-        side, partial, kept, ghost, gathered, building
-    )
+    )(c, em, kept, ends, building, sent_b, sent_a, got_b, got_a)
+    quarter = blocks // 4
+    near_groups = [[q * quarter + i for i in range(quarter)] for q in range(4)]
+    pair_groups = [[q * quarter + i, (q + 1) * quarter + i] for q in (0, 2) for i in range(quarter)]
+    half_groups = [[q * quarter + i, r * quarter + i] for q, r in ((1, 2), (0, 3)) for i in range(quarter)]
+    near = lax.all_gather(mine, "gx", axis_index_groups=near_groups)
+    (mine,) = call(condense_kernel, [mine.shape], [VMEM], 10**5, 10**5)(near)
+    pair = lax.all_gather(mine, "gx", axis_index_groups=pair_groups)
+    (mine,) = call(condense_kernel, [mine.shape], [VMEM], 10**5, 10**5)(pair)
+    half = lax.all_gather(mine, "gx", axis_index_groups=half_groups)
+    (updated,) = call(
+        finish_kernel,
+        [field],
+        [VMEM] * 7 + [SMEM],
+        10**7,
+        10**7,
+        scratch=[pltpu.VMEM(field, jnp.float32), pltpu.SemaphoreType.DMA((16,))],
+        out_space=HBM,
+    )(side, partial, kept, ghost, near, pair, half, building)
     return updated.reshape(concentration.shape)
 
 

time: 47.5 us -> 46.3 us (0.975)
  the two profiles are of different devices: /device:TPU:1 before, /device:TPU:56 now
where the time goes in v2:
time: 46.3 us; the launch traced here: 46.1 us
  blocking collectives  17.8 us (38%)
  starting transfers between devices  15.1 us (33%)
  Pallas kernels  10.1 us (22%)
  waiting for transfers between devices  2.43 us (5%)
  between operations  0.7 us (2%)
    ppermute x1, starting transfers between devices, on_device(): got_b = lax.ppermute(sent_b, 'gy', pairs_b + [(b, a) for a, b in pairs_b])  13.1 us
    all_gather x1, blocking collectives, on_device(): half = lax.all_gather(mine, 'gx', axis_index_groups=half_groups)  6.65 us
    all_gather x1, blocking collectives, on_device(): pair = lax.all_gather(mine, 'gx', axis_index_groups=pair_groups)  5.75 us
    all_gather x1, blocking collectives, on_device(): near = lax.all_gather(mine, 'gx', axis_index_groups=near_groups)  5.38 us
    pallas_call x1, Pallas kernels, on_device(): call(finish_kernel, [field], [VMEM] * 7 + [SMEM], 10 ** 7, 10 ** 7, scrat...  3.22 us
    pallas_call x1, Pallas kernels, on_device(): call(side_kernel, [field, field, (8, SUB, LANE), (7, SUB, LANE)], [VMEM]...  2.77 us
    pallas_call x1, Pallas kernels, on_device(): call(pack_kernel, [packed, packed, field] + [x.shape for x in coefs], [HB...  2.47 us
    ppermute x1, waiting for transfers between devices, on_device(): got_a = lax.ppermute(sent_a, 'gy', pairs_a + [(b, a) for a, b in pairs_a])  2.43 us
  transfers between devices with their start and end apart: 2, of which 1 were waited for; matrix products, arithmetic and copies ran while one was open for 0% of the time, Pallas kernels for 3%

profile of v2, /device:TPU:56, one launch (start us, length us, event | category | flops | bytes accessed | tf_op | source)
XLA Modules:
  0.0 46.1 jit_solution(17605919832955769369)
XLA Ops:
  0.7 2.5 %shard_map.64 = (f32[6,8,128]{2,1,0:T(8,128)S(1)}, f32[6,8,128]{2,1,0:T(8,128)S(1)}, f32[128,16,128]{2,1,0:T(8,128)S(1)}, f32[64,8,128]{2,1,0:T(8,128)S(1)}, f32...) custom-call(f32[128,16,128]{2,1,0:T(8,128)} %bitcast.14, f32[64,8,128]{2,1,0:T(8,128)} %bitcast.15, ...), custom_call_target="tpu_custom_call" | custom-call | flops 1000000 | bytes 2000000 | tf_op jit(solution)/shard_map/pallas_call | solution.py:455
  3.1 13.1 %collective-permute-start = (f32[6,8,128]{2,1,0:T(8,128)S(1)}, f32[6,8,128]{2,1,0:T(8,128)S(1)}, u32[]{:S(2)}, u32[]{:S(2)}) collective-permute-start(f32[6,8,128]{2,1,0:T(8,128)S(1)} %get-tuple-element.25.sent_b_ref), channel_id=1, source_target_pairs={{1,2},{3,4},{5,6},{7,8},{9,10},{11,12},{13,14},{15,16},{17,18},{19... | collective-permute-start | bytes 73736 | tf_op jit(solution)/shard_map/ppermute | solution.py:465
  16.3 1.9 %collective-permute-start.1 = (f32[6,8,128]{2,1,0:T(8,128)S(1)}, f32[6,8,128]{2,1,0:T(8,128)S(1)}, u32[]{:S(2)}, u32[]{:S(2)}) collective-permute-start(f32[6,8,128]{2,1,0:T(8,128)S(1)} %get-tuple-element.26.sent_a_ref), channel_id=1, source_target_pairs={{0,1},{2,3},{4,5},{6,7},{8,9},{10,11},{12,13},{14,15},{16,17},{18,... | collective-permute-start | bytes 73736 | tf_op jit(solution)/shard_map/ppermute | solution.py:466
  18.2 1.3 %shard_map.65 = (f32[128,14,8,128]{3,2,1,0:T(8,128)S(1)}, f32[2,8,128]{2,1,0:T(8,128)S(1)}) custom-call(f32[64,8,128]{2,1,0:T(8,128)S(1)} %get-tuple-element.20.cx_ref, f32[64,8,128]{2,1,0:T(8,128)S(1)} %get-tuple-element.21.cy_ref, f32[64,8,128]{2,1,0:T(8,128)S(1)} %get-tuple-element.22.vd_ref, s32[1,1]{1,0:T(1,128)S(6)} %copy.7.building_ref), custom_call_target="tpu_custom_call" | custom-call | flops 10000000 | bytes 10000000 | tf_op jit(solution)/shard_map/pallas_call | solution.py:467
  19.6 0.0 collective-permute-done.got_b_ref
  19.6 2.4 %collective-permute-done.1.got_a_ref = f32[6,8,128]{2,1,0:T(8,128)S(1)} collective-permute-done((f32[6,8,128]{2,1,0:T(8,128)S(1)}, f32[6,8,128]{2,1,0:T(8,128)S(1)}, u32[]{:S(2)}, u32[]{:S(2)}) %collective-permute-start.1) | collective-permute-done | bytes 24608 | tf_op jit(solution)/shard_map/ppermute | solution.py:466
  22.0 2.8 %shard_map.66 = (f32[128,16,128]{2,1,0:T(8,128)S(1)}, f32[128,16,128]{2,1,0:T(8,128)S(1)}, f32[8,8,128]{2,1,0:T(8,128)S(1)}, f32[7,8,128]{2,1,0:T(8,128)S(1)}) custom-call(f32[128,16,128]{2,1,0:T(8,128)S(1)} %get-tuple-element.18.c_ref, f32[64,8,128]{2,1,0:T(8,128)S(1)} %get-tuple-element.19.em_ref, f32[128,14,8,128]{3,2,1,0:T(8,128)S(1)} %get-tuple-element.23.kept_ref, ...), custom_call_target="tpu_custom_call" | custom-call | flops 10000000 | bytes 10000000 | tf_op jit(solution)/shard_map/pallas_call | solution.py:470
  24.8 5.4 %all-gather = f32[28,8,128]{2,1,0:T(8,128)S(1)} all-gather(f32[7,8,128]{2,1,0:T(8,128)S(1)} %get-tuple-element.30), channel_id=2, replica_groups={{0,32,64,96},{128,160,192,224},{256,288,320,352},{384,416,448,480},{1,3..., dimensions={0}, use_global_device_ids=true | all-gather | bytes 143360 | tf_op jit(solution)/shard_map/all_gather | solution.py:477
  30.2 0.2 shard_map.67
  30.3 5.7 %all-gather.1 = f32[14,8,128]{2,1,0:T(8,128)S(1)} all-gather(f32[7,8,128]{2,1,0:T(8,128)S(1)} %shard_map.67), channel_id=3, replica_groups={{0,128},{32,160},{64,192},{96,224},{256,384},{288,416},{320,448},{352,4..., dimensions={0}, use_global_device_ids=true | all-gather | bytes 86016 | tf_op jit(solution)/shard_map/all_gather | solution.py:479
  36.1 0.1 shard_map.68
  36.2 6.7 %all-gather.2 = f32[14,8,128]{2,1,0:T(8,128)S(1)} all-gather(f32[7,8,128]{2,1,0:T(8,128)S(1)} %shard_map.68), channel_id=4, replica_groups={{128,256},{160,288},{192,320},{224,352},{0,384},{32,416},{64,448},{96,4..., dimensions={0}, use_global_device_ids=true | all-gather | bytes 86016 | tf_op jit(solution)/shard_map/all_gather | solution.py:481
  42.9 3.2 %shard_map.69 = f32[128,16,128]{2,1,0:T(8,128)} custom-call(f32[128,16,128]{2,1,0:T(8,128)S(1)} %get-tuple-element.27.side_ref, f32[128,16,128]{2,1,0:T(8,128)S(1)} %get-tuple-element.28.partial_ref, f32[128,14,8,128]{3,2,1,0:T(8,128)S(1)} %get-tuple-element.23.kept_ref, f32[8,8,128]{2,1,0:T(8,128)S(1)} %get-tuple-element.29.ghost_ref, ...), custom_call_target="tpu_custom_call" | custom-call | flops 10000000 | bytes 10000000 | tf_op jit(solution)/shard_map/pallas_call | solution.py:482
Async XLA Ops:
  3.1 16.4 %collective-permute-start = (f32[6,8,128]{2,1,0:T(8,128)S(1)}, f32[6,8,128]{2,1,0:T(8,128)S(1)}, u32[]{:S(2)}, u32[]{:S(2)}) collective-permute-start(f32[6,8,128]{2,1,0:T(8,128)S(1)} %get-tuple-element.25.sent_b_ref), channel_id=1, source_target_pairs={{1,2},{3,4},{5,6},{7,8},{9,10},{11,12},{13,14},{15,16},{17,18},{19... | collective-permute-start | bytes 73736 | tf_op jit(solution)/shard_map/ppermute | solution.py:465
  16.3 5.7 %collective-permute-start.1 = (f32[6,8,128]{2,1,0:T(8,128)S(1)}, f32[6,8,128]{2,1,0:T(8,128)S(1)}, u32[]{:S(2)}, u32[]{:S(2)}) collective-permute-start(f32[6,8,128]{2,1,0:T(8,128)S(1)} %get-tuple-element.26.sent_a_ref), channel_id=1, source_target_pairs={{0,1},{2,3},{4,5},{6,7},{8,9},{10,11},{12,13},{14,15},{16,17},{18,... | collective-permute-start | bytes 73736 | tf_op jit(solution)/shard_map/ppermute | solution.py:466

commit v3 on v2

--- a/solution.py
+++ b/solution.py
@@ -17,7 +17,10 @@
 LIMIT = 16 * 1024 * 1024
 (INV, PULLED, FROM_PREV, WEST, EAST, CENTRE, BELOW, ABOVE, NEAR, NEAR_LOW, NEAR_UP, FAR, FAR_LOW, FAR_UP) = range(14)
 KEPT = 14
-CHUNKS = 4
+CHUNKS = 2
+PEEL = 16
+PEEL_FACTOR = 16
+PEEL_FINISH = 16
 
 
 def sub_ids():
@@ -36,6 +39,12 @@
 def subs(x, shift):
     shift %= SUB
     return pltpu.roll(x, shift, 0) if shift else x
+
+
+def stepped(body, state, peeled):
+    for k in range(peeled):
+        state = body(k, state)
+    return lax.fori_loop(peeled, 16, body, state) if peeled < 16 else state
 
 
 def fluid_of(building_ref):
@@ -63,7 +72,8 @@
 
 def neighbours(q, quads, row):
     base, offset = row
-    edge = pltpu.roll(quads[offset % 4], 126 - base - offset // 4 * 4, 1)
+    turn = 126 - base - offset // 4 * 4
+    edge = pltpu.roll(quads[offset % 4], turn, 1)
     lane = lane_ids()
     return jnp.where(lane == 0, edge, lanes(q, 1)), jnp.where(lane == LANE - 1, edge, lanes(q, -1))
 
@@ -188,7 +198,9 @@
         return ratio, from_prev, chain, first_prev
 
     zero = jnp.zeros((SUB, LANE), jnp.float32)
-    ratio, from_prev, chain, first_prev = lax.fori_loop(0, 16, rows, (zero, zero + 1.0, zero + 1.0, zero))
+    ratio, from_prev, chain, first_prev = stepped(
+        rows, (zero, zero + 1.0, zero + 1.0, zero), PEEL_FACTOR
+    )
     low = sub_ids() < 4
     ends_ref[0] = jnp.where(low, first_prev, chain)
     ends_ref[1] = jnp.where(low, from_prev, ratio)
@@ -240,7 +252,7 @@
 
 
 def side_kernel(
-    c_ref, em_ref, kept_ref, ends_ref, building_ref, sent_b_ref, sent_a_ref, got_b_ref, got_a_ref,
+    c_ref, em_ref, kept_ref, ends_ref, building_ref, sent_a_ref, sent_b_ref, got_a_ref, got_b_ref,
     side_ref, partial_ref, ghost_ref, rows_ref,
 ):
     lane, sub = lane_ids(), sub_ids()
@@ -294,7 +306,8 @@
         return last, first, chain
 
     zero = jnp.zeros((SUB, LANE), jnp.float32)
-    last, first, _ = lax.fori_loop(0, 16, rows, ([zero, zero], [zero, zero], zero + 1.0))
+    state = ([zero, zero], [zero, zero], zero + 1.0)
+    last, first, _ = stepped(rows, state, PEEL)
     rows_ref[0], rows_ref[1] = first
     rows_ref[2], rows_ref[3] = last
     rows_ref[4] = ends_ref[0]
@@ -427,7 +440,7 @@
     def written(k):
         return pltpu.make_async_copy(out_ref.at[pl.ds(8 * k, 8)], out_hbm.at[pl.ds(8 * k, 8)], sems.at[k])
 
-    lax.fori_loop(0, 16, rows, following)
+    stepped(rows, following, PEEL_FINISH)
     for k in range(16):
         written(k).wait()
 
@@ -462,14 +475,14 @@
     )(*(pltpu.with_memory_space_constraint(x, pltpu.HBM) for x in (c, *coefs)), building)
     pairs_a = [(i, i + 1) for i in range(0, devices, 2)]
     pairs_b = [(i, (i + 1) % devices) for i in range(1, devices, 2)]
+    got_a = lax.ppermute(sent_a, "gy", pairs_a + [(b, a) for a, b in pairs_a])
     got_b = lax.ppermute(sent_b, "gy", pairs_b + [(b, a) for a, b in pairs_b])
-    got_a = lax.ppermute(sent_a, "gy", pairs_a + [(b, a) for a, b in pairs_a])
     kept, ends = call(
         factor_kernel, [(cells, KEPT, SUB, LANE), (2, SUB, LANE)], [VMEM] * 3 + [SMEM], 10**7, 10**7
     )(cx, cy, vd, building)
     side, partial, ghost, mine = call(
         side_kernel, [field, field, (8, SUB, LANE), (7, SUB, LANE)], [VMEM] * 4 + [SMEM] + [VMEM] * 4, 10**7, 10**7
-    )(c, em, kept, ends, building, sent_b, sent_a, got_b, got_a)
+    )(c, em, kept, ends, building, sent_a, sent_b, got_a, got_b)
     quarter = blocks // 4
     near_groups = [[q * quarter + i for i in range(quarter)] for q in range(4)]
     pair_groups = [[q * quarter + i, (q + 1) * quarter + i] for q in (0, 2) for i in range(quarter)]

time: 46.3 us -> 42.4 us (0.916)
  Pallas kernels: 10.1 us -> 7.17 us
  waiting for transfers between devices: 2.43 us -> 0.63 us
  starting transfers between devices: 15.1 us -> 15.9 us
    ppermute x1, waiting for transfers between devices: 2.43 us -> 0.01 us  [on_device(): got_a = lax.ppermute(sent_a, 'gy', pairs_a + [(b, a) for a, b in pairs_a])]
    pallas_call x1, Pallas kernels: 2.77 us -> 1.14 us  [on_device(): call(side_kernel, [field, field, (8, SUB, LANE), (7, SUB, LANE)], [VMEM]...]
    ppermute x1, starting transfers between devices: 1.92 us -> 3.4 us  [on_device(): got_a = lax.ppermute(sent_a, 'gy', pairs_a + [(b, a) for a, b in pairs_a])]
    pallas_call x1, Pallas kernels: 3.22 us -> 2.16 us  [on_device(): call(finish_kernel, [field], [VMEM] * 7 + [SMEM], 10 ** 7, 10 ** 7, scrat...]
    ppermute x1, starting transfers between devices: 13.1 us -> 12.5 us  [on_device(): got_b = lax.ppermute(sent_b, 'gy', pairs_b + [(b, a) for a, b in pairs_b])]
    ppermute x1, waiting for transfers between devices: 0.01 us -> 0.62 us  [on_device(): got_b = lax.ppermute(sent_b, 'gy', pairs_b + [(b, a) for a, b in pairs_b])]
where the time goes in v3:
time: 42.4 us; the launch traced here: 42.2 us
  blocking collectives  17.8 us (42%)
  starting transfers between devices  15.9 us (38%)
  Pallas kernels  7.17 us (17%)
  between operations  0.7 us (2%)
  waiting for transfers between devices  0.63 us (1%)
    ppermute x1, starting transfers between devices, on_device(): got_b = lax.ppermute(sent_b, 'gy', pairs_b + [(b, a) for a, b in pairs_b])  12.5 us
    all_gather x1, blocking collectives, on_device(): half = lax.all_gather(mine, 'gx', axis_index_groups=half_groups)  6.65 us
    all_gather x1, blocking collectives, on_device(): pair = lax.all_gather(mine, 'gx', axis_index_groups=pair_groups)  5.75 us
    all_gather x1, blocking collectives, on_device(): near = lax.all_gather(mine, 'gx', axis_index_groups=near_groups)  5.38 us
    ppermute x1, starting transfers between devices, on_device(): got_a = lax.ppermute(sent_a, 'gy', pairs_a + [(b, a) for a, b in pairs_a])  3.4 us
    pallas_call x1, Pallas kernels, on_device(): call(pack_kernel, [packed, packed, field] + [x.shape for x in coefs], [HB...  2.41 us
    pallas_call x1, Pallas kernels, on_device(): call(finish_kernel, [field], [VMEM] * 7 + [SMEM], 10 ** 7, 10 ** 7, scrat...  2.16 us
    pallas_call x1, Pallas kernels, on_device(): call(factor_kernel, [(cells, KEPT, SUB, LANE), (2, SUB, LANE)], [VMEM] *...  1.14 us
  transfers between devices with their start and end apart: 2, of which 1 were waited for; matrix products, arithmetic and copies ran while one was open for 0% of the time, Pallas kernels for 3%

profile of v3, /device:TPU:56, one launch (start us, length us, event | category | flops | bytes accessed | tf_op | source)
XLA Modules:
  0.0 42.2 jit_solution(15854620112474093507)
XLA Ops:
  0.7 2.4 %shard_map.64 = (f32[6,8,128]{2,1,0:T(8,128)S(1)}, f32[6,8,128]{2,1,0:T(8,128)S(1)}, f32[128,16,128]{2,1,0:T(8,128)S(1)}, f32[64,8,128]{2,1,0:T(8,128)S(1)}, f32...) custom-call(f32[128,16,128]{2,1,0:T(8,128)} %bitcast.14, f32[64,8,128]{2,1,0:T(8,128)} %bitcast.15, ...), custom_call_target="tpu_custom_call" | custom-call | flops 1000000 | bytes 2000000 | tf_op jit(solution)/shard_map/pallas_call | solution.py:468
  3.1 3.4 %collective-permute-start = (f32[6,8,128]{2,1,0:T(8,128)S(1)}, f32[6,8,128]{2,1,0:T(8,128)S(1)}, u32[]{:S(2)}, u32[]{:S(2)}) collective-permute-start(f32[6,8,128]{2,1,0:T(8,128)S(1)} %get-tuple-element.25.sent_a_ref), channel_id=1, source_target_pairs={{0,1},{2,3},{4,5},{6,7},{8,9},{10,11},{12,13},{14,15},{16,17},{18,... | collective-permute-start | bytes 73736 | tf_op jit(solution)/shard_map/ppermute | solution.py:478
  6.5 12.5 %collective-permute-start.1 = (f32[6,8,128]{2,1,0:T(8,128)S(1)}, f32[6,8,128]{2,1,0:T(8,128)S(1)}, u32[]{:S(2)}, u32[]{:S(2)}) collective-permute-start(f32[6,8,128]{2,1,0:T(8,128)S(1)} %get-tuple-element.26.sent_b_ref), channel_id=1, source_target_pairs={{1,2},{3,4},{5,6},{7,8},{9,10},{11,12},{13,14},{15,16},{17,18},{19... | collective-permute-start | bytes 73736 | tf_op jit(solution)/shard_map/ppermute | solution.py:479
  19.0 1.1 %shard_map.65 = (f32[128,14,8,128]{3,2,1,0:T(8,128)S(1)}, f32[2,8,128]{2,1,0:T(8,128)S(1)}) custom-call(f32[64,8,128]{2,1,0:T(8,128)S(1)} %get-tuple-element.20.cx_ref, f32[64,8,128]{2,1,0:T(8,128)S(1)} %get-tuple-element.21.cy_ref, f32[64,8,128]{2,1,0:T(8,128)S(1)} %get-tuple-element.22.vd_ref, s32[1,1]{1,0:T(1,128)S(6)} %copy.7.building_ref), custom_call_target="tpu_custom_call" | custom-call | flops 10000000 | bytes 10000000 | tf_op jit(solution)/shard_map/pallas_call | solution.py:480
  20.1 0.0 collective-permute-done.got_a_ref
  20.1 0.6 %collective-permute-done.1.got_b_ref = f32[6,8,128]{2,1,0:T(8,128)S(1)} collective-permute-done((f32[6,8,128]{2,1,0:T(8,128)S(1)}, f32[6,8,128]{2,1,0:T(8,128)S(1)}, u32[]{:S(2)}, u32[]{:S(2)}) %collective-permute-start.1) | collective-permute-done | bytes 24608 | tf_op jit(solution)/shard_map/ppermute | solution.py:479
  20.8 1.1 %shard_map.66 = (f32[128,16,128]{2,1,0:T(8,128)S(1)}, f32[128,16,128]{2,1,0:T(8,128)S(1)}, f32[8,8,128]{2,1,0:T(8,128)S(1)}, f32[7,8,128]{2,1,0:T(8,128)S(1)}) custom-call(f32[128,16,128]{2,1,0:T(8,128)S(1)} %get-tuple-element.18.c_ref, f32[64,8,128]{2,1,0:T(8,128)S(1)} %get-tuple-element.19.em_ref, f32[128,14,8,128]{3,2,1,0:T(8,128)S(1)} %get-tuple-element.23.kept_ref, ...), custom_call_target="tpu_custom_call" | custom-call | flops 10000000 | bytes 10000000 | tf_op jit(solution)/shard_map/pallas_call | solution.py:483
  21.9 5.4 %all-gather = f32[28,8,128]{2,1,0:T(8,128)S(1)} all-gather(f32[7,8,128]{2,1,0:T(8,128)S(1)} %get-tuple-element.30), channel_id=2, replica_groups={{0,32,64,96},{128,160,192,224},{256,288,320,352},{384,416,448,480},{1,3..., dimensions={0}, use_global_device_ids=true | all-gather | bytes 143360 | tf_op jit(solution)/shard_map/all_gather | solution.py:490
  27.3 0.2 shard_map.67
  27.4 5.7 %all-gather.1 = f32[14,8,128]{2,1,0:T(8,128)S(1)} all-gather(f32[7,8,128]{2,1,0:T(8,128)S(1)} %shard_map.67), channel_id=3, replica_groups={{0,128},{32,160},{64,192},{96,224},{256,384},{288,416},{320,448},{352,4..., dimensions={0}, use_global_device_ids=true | all-gather | bytes 86016 | tf_op jit(solution)/shard_map/all_gather | solution.py:492
  33.2 0.1 shard_map.68
  33.3 6.7 %all-gather.2 = f32[14,8,128]{2,1,0:T(8,128)S(1)} all-gather(f32[7,8,128]{2,1,0:T(8,128)S(1)} %shard_map.68), channel_id=4, replica_groups={{128,256},{160,288},{192,320},{224,352},{0,384},{32,416},{64,448},{96,4..., dimensions={0}, use_global_device_ids=true | all-gather | bytes 86016 | tf_op jit(solution)/shard_map/all_gather | solution.py:494
  40.0 2.2 %shard_map.69 = f32[128,16,128]{2,1,0:T(8,128)} custom-call(f32[128,16,128]{2,1,0:T(8,128)S(1)} %get-tuple-element.27.side_ref, f32[128,16,128]{2,1,0:T(8,128)S(1)} %get-tuple-element.28.partial_ref, f32[128,14,8,128]{3,2,1,0:T(8,128)S(1)} %get-tuple-element.23.kept_ref, f32[8,8,128]{2,1,0:T(8,128)S(1)} %get-tuple-element.29.ghost_ref, ...), custom_call_target="tpu_custom_call" | custom-call | flops 10000000 | bytes 10000000 | tf_op jit(solution)/shard_map/pallas_call | solution.py:495
Async XLA Ops:
  3.1 17.1 %collective-permute-start = (f32[6,8,128]{2,1,0:T(8,128)S(1)}, f32[6,8,128]{2,1,0:T(8,128)S(1)}, u32[]{:S(2)}, u32[]{:S(2)}) collective-permute-start(f32[6,8,128]{2,1,0:T(8,128)S(1)} %get-tuple-element.25.sent_a_ref), channel_id=1, source_target_pairs={{0,1},{2,3},{4,5},{6,7},{8,9},{10,11},{12,13},{14,15},{16,17},{18,... | collective-permute-start | bytes 73736 | tf_op jit(solution)/shard_map/ppermute | solution.py:478
  6.5 14.3 %collective-permute-start.1 = (f32[6,8,128]{2,1,0:T(8,128)S(1)}, f32[6,8,128]{2,1,0:T(8,128)S(1)}, u32[]{:S(2)}, u32[]{:S(2)}) collective-permute-start(f32[6,8,128]{2,1,0:T(8,128)S(1)} %get-tuple-element.26.sent_b_ref), channel_id=1, source_target_pairs={{1,2},{3,4},{5,6},{7,8},{9,10},{11,12},{13,14},{15,16},{17,18},{19... | collective-permute-start | bytes 73736 | tf_op jit(solution)/shard_map/ppermute | solution.py:479

commit v4 on v3

--- a/solution.py
+++ b/solution.py
@@ -13,6 +13,7 @@
 SUB, LANE = 8, 128
 VMEM = pl.BlockSpec(memory_space=pltpu.VMEM)
 HBM = pl.BlockSpec(memory_space=pltpu.HBM)
+ANY = pl.BlockSpec(memory_space=pl.ANY)
 SMEM = pl.BlockSpec(memory_space=pltpu.SMEM)
 LIMIT = 16 * 1024 * 1024
 (INV, PULLED, FROM_PREV, WEST, EAST, CENTRE, BELOW, ABOVE, NEAR, NEAR_LOW, NEAR_UP, FAR, FAR_LOW, FAR_UP) = range(14)
@@ -148,7 +149,7 @@
         b_ref[n] = jnp.where(even_gy, to_left, to_right)
 
 
-def factor_kernel(cx_ref, cy_ref, vd_ref, building_ref, kept_ref, ends_ref):
+def factor_kernel(cx_ref, cy_ref, vd_ref, building_ref, early_ref, kept_ref, ends_ref):
     fluid = fluid_of(building_ref)
     push = cross_diff * fluid
     ground = sub_ids() % 4 == 0
@@ -252,7 +253,7 @@
 
 
 def side_kernel(
-    c_ref, em_ref, kept_ref, ends_ref, building_ref, sent_a_ref, sent_b_ref, got_a_ref, got_b_ref,
+    c_ref, em_ref, kept_ref, ends_ref, building_ref, sent_a_ref, sent_b_ref, got_early_ref, got_b_ref, got_late_ref,
     side_ref, partial_ref, ghost_ref, rows_ref,
 ):
     lane, sub = lane_ids(), sub_ids()
@@ -261,8 +262,10 @@
     even_gy = lax.rem(lax.axis_index("gy"), 2) == 0
     own_left = [jnp.where(even_gy, sent_b_ref[n], sent_a_ref[n]) for n in range(2)]
     own_right = [jnp.where(even_gy, sent_a_ref[n], sent_b_ref[n]) for n in range(2)]
-    from_left = [jnp.where(even_gy, got_b_ref[n], got_a_ref[n]) for n in range(6)]
-    from_right = [jnp.where(even_gy, got_a_ref[n], got_b_ref[n]) for n in range(6)]
+    early = lax.axis_index("gy") < lax.axis_size("gy") // 4 * 2
+    got_a = [jnp.where(early, got_early_ref[n], got_late_ref[n]) for n in range(6)]
+    from_left = [jnp.where(even_gy, got_b_ref[n], got_a[n]) for n in range(6)]
+    from_right = [jnp.where(even_gy, got_a[n], got_b_ref[n]) for n in range(6)]
 
     extra = jnp.zeros((SUB, LANE), jnp.float32)
     for s, parts in enumerate(ghost_columns(from_left, from_right, own_left, own_right)):
@@ -473,16 +476,20 @@
         2 * 10**6,
         scratch=[pltpu.SemaphoreType.DMA((CHUNKS + 4,))],
     )(*(pltpu.with_memory_space_constraint(x, pltpu.HBM) for x in (c, *coefs)), building)
-    pairs_a = [(i, i + 1) for i in range(0, devices, 2)]
-    pairs_b = [(i, (i + 1) % devices) for i in range(1, devices, 2)]
-    got_a = lax.ppermute(sent_a, "gy", pairs_a + [(b, a) for a, b in pairs_a])
-    got_b = lax.ppermute(sent_b, "gy", pairs_b + [(b, a) for a, b in pairs_b])
+    half = devices // 4 * 2
+    even = [(i, i + 1) for i in range(0, devices, 2)]
+    odd = [(i, (i + 1) % devices) for i in range(1, devices, 2)]
+    low, high = [p for p in even if p[0] < half], [p for p in even if p[0] >= half]
+    got_early, got_b, got_late = (
+        lax.ppermute(sent, "gy", pairs + [(b, a) for a, b in pairs])
+        for sent, pairs in ((sent_a, low), (sent_b, odd), (sent_a, high))
+    )
     kept, ends = call(
-        factor_kernel, [(cells, KEPT, SUB, LANE), (2, SUB, LANE)], [VMEM] * 3 + [SMEM], 10**7, 10**7
-    )(cx, cy, vd, building)
+        factor_kernel, [(cells, KEPT, SUB, LANE), (2, SUB, LANE)], [VMEM] * 3 + [SMEM, ANY], 10**7, 10**7
+    )(cx, cy, vd, building, got_early)
     side, partial, ghost, mine = call(
-        side_kernel, [field, field, (8, SUB, LANE), (7, SUB, LANE)], [VMEM] * 4 + [SMEM] + [VMEM] * 4, 10**7, 10**7
-    )(c, em, kept, ends, building, sent_a, sent_b, got_a, got_b)
+        side_kernel, [field, field, (8, SUB, LANE), (7, SUB, LANE)], [VMEM] * 4 + [SMEM] + [VMEM] * 5, 10**7, 10**7
+    )(c, em, kept, ends, building, sent_a, sent_b, got_early, got_b, got_late)
     quarter = blocks // 4
     near_groups = [[q * quarter + i for i in range(quarter)] for q in range(4)]
     pair_groups = [[q * quarter + i, (q + 1) * quarter + i] for q in (0, 2) for i in range(quarter)]

time: 42.4 us -> 40.4 us (0.953)
  starting transfers between devices: 15.9 us -> 14.5 us
  waiting for transfers between devices: 0.63 us -> 0.01 us
    ppermute x2 -> x3, starting transfers between devices: 15.9 us -> 14.5 us  [on_device(): lax.ppermute(sent, 'gy', pairs + [(b, a) for a, b in pairs])]
    ppermute x2 -> x3, waiting for transfers between devices: 0.63 us -> 0.01 us  [on_device(): lax.ppermute(sent, 'gy', pairs + [(b, a) for a, b in pairs])]
  transfers between devices with their start and end apart: 2 -> 3, of which waited for: 1 -> 0; matrix products, arithmetic and copies ran while one was open for 0% -> 0% of each run, Pallas kernels for 3% -> 3%
where the time goes in v4:
time: 40.4 us; the launch traced here: 40.2 us
  blocking collectives  17.8 us (44%)
  starting transfers between devices  14.5 us (36%)
  Pallas kernels  7.2 us (18%)
  between operations  0.72 us (2%)
    ppermute x3, starting transfers between devices, on_device(): lax.ppermute(sent, 'gy', pairs + [(b, a) for a, b in pairs])  14.5 us
    all_gather x1, blocking collectives, on_device(): half = lax.all_gather(mine, 'gx', axis_index_groups=half_groups)  6.65 us
    all_gather x1, blocking collectives, on_device(): pair = lax.all_gather(mine, 'gx', axis_index_groups=pair_groups)  5.75 us
    all_gather x1, blocking collectives, on_device(): near = lax.all_gather(mine, 'gx', axis_index_groups=near_groups)  5.38 us
    pallas_call x1, Pallas kernels, on_device(): call(pack_kernel, [packed, packed, field] + [x.shape for x in coefs], [HB...  2.41 us
    pallas_call x1, Pallas kernels, on_device(): call(finish_kernel, [field], [VMEM] * 7 + [SMEM], 10 ** 7, 10 ** 7, scrat...  2.17 us
    pallas_call x1, Pallas kernels, on_device(): call(side_kernel, [field, field, (8, SUB, LANE), (7, SUB, LANE)], [VMEM]...  1.16 us
    pallas_call x1, Pallas kernels, on_device(): call(factor_kernel, [(cells, KEPT, SUB, LANE), (2, SUB, LANE)], [VMEM] *...  1.14 us
  transfers between devices with their start and end apart: 3, of which 0 were waited for; matrix products, arithmetic and copies ran while one was open for 0% of the time, Pallas kernels for 3%

profile of v4, /device:TPU:56, one launch (start us, length us, event | category | flops | bytes accessed | tf_op | source)
XLA Modules:
  0.0 40.2 jit_solution(4449102187413091893)
XLA Ops:
  0.7 2.4 %shard_map.64 = (f32[6,8,128]{2,1,0:T(8,128)S(1)}, f32[6,8,128]{2,1,0:T(8,128)S(1)}, f32[128,16,128]{2,1,0:T(8,128)S(1)}, f32[64,8,128]{2,1,0:T(8,128)S(1)}, f32...) custom-call(f32[128,16,128]{2,1,0:T(8,128)} %bitcast.14, f32[64,8,128]{2,1,0:T(8,128)} %bitcast.15, ...), custom_call_target="tpu_custom_call" | custom-call | flops 1000000 | bytes 2000000 | tf_op jit(solution)/shard_map/pallas_call | solution.py:471
  3.1 3.4 %collective-permute-start = (f32[6,8,128]{2,1,0:T(8,128)S(1)}, f32[6,8,128]{2,1,0:T(8,128)S(1)}, u32[]{:S(2)}, u32[]{:S(2)}) collective-permute-start(f32[6,8,128]{2,1,0:T(8,128)S(1)} %get-tuple-element.23.sent_a_ref), channel_id=1, source_target_pairs={{0,1},{2,3},{4,5},{6,7},{8,9},{10,11},{12,13},{14,15},{1,0},{3,2},... | collective-permute-start | bytes 73736 | tf_op jit(solution)/shard_map/ppermute | solution.py:484
  6.5 10.4 %collective-permute-start.1 = (f32[6,8,128]{2,1,0:T(8,128)S(1)}, f32[6,8,128]{2,1,0:T(8,128)S(1)}, u32[]{:S(2)}, u32[]{:S(2)}) collective-permute-start(f32[6,8,128]{2,1,0:T(8,128)S(1)} %get-tuple-element.26.sent_b_ref), channel_id=1, source_target_pairs={{1,2},{3,4},{5,6},{7,8},{9,10},{11,12},{13,14},{15,16},{17,18},{19... | collective-permute-start | bytes 73736 | tf_op jit(solution)/shard_map/ppermute | solution.py:484
  16.9 0.7 %collective-permute-start.2 = (f32[6,8,128]{2,1,0:T(8,128)S(1)}, f32[6,8,128]{2,1,0:T(8,128)S(1)}, u32[]{:S(2)}, u32[]{:S(2)}) collective-permute-start(f32[6,8,128]{2,1,0:T(8,128)S(1)} %get-tuple-element.23.sent_a_ref), channel_id=1, source_target_pairs={{16,17},{18,19},{20,21},{22,23},{24,25},{26,27},{28,29},{30,31},{1... | collective-permute-start | bytes 73736 | tf_op jit(solution)/shard_map/ppermute | solution.py:484
  17.6 0.0 collective-permute-done.early_ref.got_early_ref
  17.6 1.1 %shard_map.65 = (f32[128,14,8,128]{3,2,1,0:T(8,128)S(1)}, f32[2,8,128]{2,1,0:T(8,128)S(1)}) custom-call(f32[64,8,128]{2,1,0:T(8,128)S(1)} %get-tuple-element.20.cx_ref, f32[64,8,128]{2,1,0:T(8,128)S(1)} %get-tuple-element.21.cy_ref, f32[64,8,128]{2,1,0:T(8,128)S(1)} %get-tuple-element.22.vd_ref, s32[1,1]{1,0:T(1,128)S(6)} %copy.7.building_ref, ...), custom_call_target="tpu_custom_call" | custom-call | flops 10000000 | bytes 10000000 | tf_op jit(solution)/shard_map/pallas_call | solution.py:487
  18.7 0.0 collective-permute-done.1.got_b_ref
  18.7 0.0 collective-permute-done.2.got_late_ref
  18.7 1.2 %shard_map.66 = (f32[128,16,128]{2,1,0:T(8,128)S(1)}, f32[128,16,128]{2,1,0:T(8,128)S(1)}, f32[8,8,128]{2,1,0:T(8,128)S(1)}, f32[7,8,128]{2,1,0:T(8,128)S(1)}) custom-call(f32[128,16,128]{2,1,0:T(8,128)S(1)} %get-tuple-element.18.c_ref, f32[64,8,128]{2,1,0:T(8,128)S(1)} %get-tuple-element.19.em_ref, f32[128,14,8,128]{3,2,1,0:T(8,128)S(1)} %get-tuple-element.24.kept_ref, ...), custom_call_target="tpu_custom_call" | custom-call | flops 10000000 | bytes 10000000 | tf_op jit(solution)/shard_map/pallas_call | solution.py:490
  19.9 5.4 %all-gather = f32[28,8,128]{2,1,0:T(8,128)S(1)} all-gather(f32[7,8,128]{2,1,0:T(8,128)S(1)} %get-tuple-element.30), channel_id=2, replica_groups={{0,32,64,96},{128,160,192,224},{256,288,320,352},{384,416,448,480},{1,3..., dimensions={0}, use_global_device_ids=true | all-gather | bytes 143360 | tf_op jit(solution)/shard_map/all_gather | solution.py:497
  25.3 0.2 shard_map.67
  25.5 5.7 %all-gather.1 = f32[14,8,128]{2,1,0:T(8,128)S(1)} all-gather(f32[7,8,128]{2,1,0:T(8,128)S(1)} %shard_map.67), channel_id=3, replica_groups={{0,128},{32,160},{64,192},{96,224},{256,384},{288,416},{320,448},{352,4..., dimensions={0}, use_global_device_ids=true | all-gather | bytes 86016 | tf_op jit(solution)/shard_map/all_gather | solution.py:499
  31.2 0.1 shard_map.68
  31.4 6.7 %all-gather.2 = f32[14,8,128]{2,1,0:T(8,128)S(1)} all-gather(f32[7,8,128]{2,1,0:T(8,128)S(1)} %shard_map.68), channel_id=4, replica_groups={{128,256},{160,288},{192,320},{224,352},{0,384},{32,416},{64,448},{96,4..., dimensions={0}, use_global_device_ids=true | all-gather | bytes 86016 | tf_op jit(solution)/shard_map/all_gather | solution.py:501
  38.0 2.2 %shard_map.69 = f32[128,16,128]{2,1,0:T(8,128)} custom-call(f32[128,16,128]{2,1,0:T(8,128)S(1)} %get-tuple-element.27.side_ref, f32[128,16,128]{2,1,0:T(8,128)S(1)} %get-tuple-element.28.partial_ref, f32[128,14,8,128]{3,2,1,0:T(8,128)S(1)} %get-tuple-element.24.kept_ref, f32[8,8,128]{2,1,0:T(8,128)S(1)} %get-tuple-element.29.ghost_ref, ...), custom_call_target="tpu_custom_call" | custom-call | flops 10000000 | bytes 10000000 | tf_op jit(solution)/shard_map/pallas_call | solution.py:502
Async XLA Ops:
  3.1 14.5 %collective-permute-start = (f32[6,8,128]{2,1,0:T(8,128)S(1)}, f32[6,8,128]{2,1,0:T(8,128)S(1)}, u32[]{:S(2)}, u32[]{:S(2)}) collective-permute-start(f32[6,8,128]{2,1,0:T(8,128)S(1)} %get-tuple-element.23.sent_a_ref), channel_id=1, source_target_pairs={{0,1},{2,3},{4,5},{6,7},{8,9},{10,11},{12,13},{14,15},{1,0},{3,2},... | collective-permute-start | bytes 73736 | tf_op jit(solution)/shard_map/ppermute | solution.py:484
  6.5 12.3 %collective-permute-start.1 = (f32[6,8,128]{2,1,0:T(8,128)S(1)}, f32[6,8,128]{2,1,0:T(8,128)S(1)}, u32[]{:S(2)}, u32[]{:S(2)}) collective-permute-start(f32[6,8,128]{2,1,0:T(8,128)S(1)} %get-tuple-element.26.sent_b_ref), channel_id=1, source_target_pairs={{1,2},{3,4},{5,6},{7,8},{9,10},{11,12},{13,14},{15,16},{17,18},{19... | collective-permute-start | bytes 73736 | tf_op jit(solution)/shard_map/ppermute | solution.py:484
  16.9 1.9 %collective-permute-start.2 = (f32[6,8,128]{2,1,0:T(8,128)S(1)}, f32[6,8,128]{2,1,0:T(8,128)S(1)}, u32[]{:S(2)}, u32[]{:S(2)}) collective-permute-start(f32[6,8,128]{2,1,0:T(8,128)S(1)} %get-tuple-element.23.sent_a_ref), channel_id=1, source_target_pairs={{16,17},{18,19},{20,21},{22,23},{24,25},{26,27},{28,29},{30,31},{1... | collective-permute-start | bytes 73736 | tf_op jit(solution)/shard_map/ppermute | solution.py:484

commit v5 on v4

--- a/solution.py
+++ b/solution.py
@@ -18,7 +18,7 @@
 LIMIT = 16 * 1024 * 1024
 (INV, PULLED, FROM_PREV, WEST, EAST, CENTRE, BELOW, ABOVE, NEAR, NEAR_LOW, NEAR_UP, FAR, FAR_LOW, FAR_UP) = range(14)
 KEPT = 14
-CHUNKS = 2
+CHUNKS = 1
 PEEL = 16
 PEEL_FACTOR = 16
 PEEL_FINISH = 16
@@ -90,7 +90,7 @@
         for n in range(CHUNKS)
     ]
     copies += [pltpu.make_async_copy(src, dst, sems.at[CHUNKS + n]) for n, (src, dst) in enumerate(coefs)]
-    for copy in copies:
+    for copy in copies[CHUNKS:] + copies[:CHUNKS]:
         copy.start()
 
     lane, sub = lane_ids(), sub_ids()
@@ -99,6 +99,19 @@
     even_gy = lax.rem(lax.axis_index("gy"), 2) == 0
     quarter = lane // 4
     zero = jnp.zeros((SUB, LANE), jnp.float32)
+    even = lane % 2 == 0
+    pair_of = lane // 2
+    first, last = [], []
+    for n, (_, ref) in enumerate(coefs):
+        copies[CHUNKS + n].wait()
+        acc = zero
+        for k in range(64):
+            acc = jnp.where(pair_of == k, lanes(ref[k], 2 * k + 1), acc)
+        turned = subs(acc, 4)
+        at_even = jnp.where(low, acc, turned)
+        at_odd = jnp.where(low, turned, acc)
+        last.append(jnp.where(even, at_even, lanes(at_odd, 1)))
+        first.append(jnp.where(even, lanes(at_even, -1), at_odd))
     picked = [[zero] * 4 for _ in range(2)]
     for n in range(CHUNKS):
         copies[n].wait()
@@ -117,19 +130,6 @@
                 out = jnp.where(lane % 4 == g, lanes(picked[half][g], g - j), out)
             found.append(out)
         columns.append(found)
-    even = lane % 2 == 0
-    pair_of = lane // 2
-    first, last = [], []
-    for n, (_, ref) in enumerate(coefs):
-        copies[CHUNKS + n].wait()
-        acc = zero
-        for k in range(64):
-            acc = jnp.where(pair_of == k, lanes(ref[k], 2 * k + 1), acc)
-        turned = subs(acc, 4)
-        at_even = jnp.where(low, acc, turned)
-        at_odd = jnp.where(low, turned, acc)
-        last.append(jnp.where(even, at_even, lanes(at_odd, 1)))
-        first.append(jnp.where(even, lanes(at_even, -1), at_odd))
     sides = []
     for (outer, inner), edge in (((2, 3), first), ((1, 0), last)):
         pull = fluid * (edge[0] + cross_diff)
@@ -363,6 +363,34 @@
     out_ref[6] = packed
 
 
+def half_kernel(rows_ref, out_ref):
+    main, extra = (functools.reduce(joined, forms) for forms in blocks_of(rows_ref))
+    lane = lane_ids()
+    lower = lax.axis_index("gx") < lax.axis_size("gx") // 2
+
+    def facing(form):
+        first, last, first_prev, _, _, last_next = form
+        own = [jnp.where(lower, last[h], first[h]) for h in range(2)]
+        return (*own, jnp.where(lower, last_next, first_prev))
+
+    for n, part in enumerate(facing(main)):
+        out_ref[n] = part
+    parts = facing(extra)
+    packed = parts[0]
+    for j in (1, 2):
+        packed = jnp.where(lane // 2 == j, lanes(parts[j], 2 * j), packed)
+    out_ref[3] = packed
+
+
+def halves(lower_side, upper_side, lower):
+    last, last_next = lower_side[0:2], lower_side[2]
+    first, first_prev = upper_side[0:2], upper_side[2]
+    inv = 1.0 / (1.0 - last_next * first_prev)
+    ends = [(last[h] + last_next * first[h]) * inv for h in range(2)]
+    starts = [first[h] + first_prev * ends[h] for h in range(2)]
+    return [jnp.where(lower, 0.0, ends[h]) for h in range(2)], [jnp.where(lower, starts[h], 0.0) for h in range(2)]
+
+
 def interface(blocks, place, before, beyond):
     zero = jnp.zeros((SUB, LANE), jnp.float32)
     own, slope = before, zero
@@ -397,12 +425,10 @@
     push = cross_diff * fluid_of(building_ref)
     place = lax.axis_index("gx")
     quarter = near_ref.shape[0]
-    zero = jnp.zeros((SUB, LANE), jnp.float32)
-    preceding, following = [zero, zero], [zero, zero]
-    ghost_prev, ghost_next = preceding, following
-    for ref, at in (
-        (half_ref, place // (2 * quarter)), (pair_ref, place // quarter % 2), (near_ref, place % quarter)
-    ):
+    lower = place < lax.axis_size("gx") // 2
+    preceding, following = halves(*([half_ref[k, n] for n in range(3)] for k in range(2)), lower)
+    ghost_prev, ghost_next = halves(*([lanes(half_ref[k, 3], -2 * n) for n in range(3)] for k in range(2)), lower)
+    for ref, at in ((pair_ref, place // quarter % 2), (near_ref, place % quarter)):
         main, extra = blocks_of(ref)
         preceding, following = interface(main, at, preceding, following)
         ghost_prev, ghost_next = interface(extra, at, ghost_prev, ghost_next)
@@ -492,12 +518,12 @@
     )(c, em, kept, ends, building, sent_a, sent_b, got_early, got_b, got_late)
     quarter = blocks // 4
     near_groups = [[q * quarter + i for i in range(quarter)] for q in range(4)]
-    pair_groups = [[q * quarter + i, (q + 1) * quarter + i] for q in (0, 2) for i in range(quarter)]
-    half_groups = [[q * quarter + i, r * quarter + i] for q, r in ((1, 2), (0, 3)) for i in range(quarter)]
+    pair_groups = [[q * quarter + i, (q + 1) * quarter + (i + quarter // 2) % quarter] for q in (0, 2) for i in range(quarter)]
+    half_groups = [[q * quarter + i, r * quarter + (i + quarter // 2) % quarter] for q, r in ((1, 2), (0, 3)) for i in range(quarter)]
     near = lax.all_gather(mine, "gx", axis_index_groups=near_groups)
     (mine,) = call(condense_kernel, [mine.shape], [VMEM], 10**5, 10**5)(near)
     pair = lax.all_gather(mine, "gx", axis_index_groups=pair_groups)
-    (mine,) = call(condense_kernel, [mine.shape], [VMEM], 10**5, 10**5)(pair)
+    (mine,) = call(half_kernel, [(4, SUB, LANE)], [VMEM], 10**5, 10**5)(pair)
     half = lax.all_gather(mine, "gx", axis_index_groups=half_groups)
     (updated,) = call(
         finish_kernel,

time: 40.4 us -> 39.8 us (0.985)
    all_gather x1, blocking collectives: 6.65 us -> 5.68 us  [on_device(): half = lax.all_gather(mine, 'gx', axis_index_groups=half_groups)]
    all_gather x1, blocking collectives: 5.75 us -> 6.34 us  [on_device(): pair = lax.all_gather(mine, 'gx', axis_index_groups=pair_groups)]
where the time goes in v5:
time: 39.8 us; the launch traced here: 39.6 us
  blocking collectives  17.4 us (44%)
  starting transfers between devices  14.5 us (36%)
  Pallas kernels  7.01 us (18%)
  between operations  0.72 us (2%)
    ppermute x3, starting transfers between devices, on_device(): lax.ppermute(sent, 'gy', pairs + [(b, a) for a, b in pairs])  14.5 us
    all_gather x1, blocking collectives, on_device(): pair = lax.all_gather(mine, 'gx', axis_index_groups=pair_groups)  6.34 us
    all_gather x1, blocking collectives, on_device(): half = lax.all_gather(mine, 'gx', axis_index_groups=half_groups)  5.68 us
    all_gather x1, blocking collectives, on_device(): near = lax.all_gather(mine, 'gx', axis_index_groups=near_groups)  5.38 us
    pallas_call x1, Pallas kernels, on_device(): call(pack_kernel, [packed, packed, field] + [x.shape for x in coefs], [HB...  2.24 us
    pallas_call x1, Pallas kernels, on_device(): call(finish_kernel, [field], [VMEM] * 7 + [SMEM], 10 ** 7, 10 ** 7, scrat...  2.15 us
    pallas_call x1, Pallas kernels, on_device(): call(side_kernel, [field, field, (8, SUB, LANE), (7, SUB, LANE)], [VMEM]...  1.16 us
    pallas_call x1, Pallas kernels, on_device(): call(factor_kernel, [(cells, KEPT, SUB, LANE), (2, SUB, LANE)], [VMEM] *...  1.14 us
  transfers between devices with their start and end apart: 3, of which 0 were waited for; matrix products, arithmetic and copies ran while one was open for 0% of the time, Pallas kernels for 3%

profile of v5, /device:TPU:56, one launch (start us, length us, event | category | flops | bytes accessed | tf_op | source)
XLA Modules:
  0.0 39.6 jit_solution(6603116291364282933)
XLA Ops:
  0.7 2.2 %shard_map.64 = (f32[6,8,128]{2,1,0:T(8,128)S(1)}, f32[6,8,128]{2,1,0:T(8,128)S(1)}, f32[128,16,128]{2,1,0:T(8,128)S(1)}, f32[64,8,128]{2,1,0:T(8,128)S(1)}, f32...) custom-call(f32[128,16,128]{2,1,0:T(8,128)} %bitcast.14, f32[64,8,128]{2,1,0:T(8,128)} %bitcast.15, ...), custom_call_target="tpu_custom_call" | custom-call | flops 1000000 | bytes 2000000 | tf_op jit(solution)/shard_map/pallas_call | solution.py:497
  2.9 3.4 %collective-permute-start = (f32[6,8,128]{2,1,0:T(8,128)S(1)}, f32[6,8,128]{2,1,0:T(8,128)S(1)}, u32[]{:S(2)}, u32[]{:S(2)}) collective-permute-start(f32[6,8,128]{2,1,0:T(8,128)S(1)} %get-tuple-element.23.sent_a_ref), channel_id=1, source_target_pairs={{0,1},{2,3},{4,5},{6,7},{8,9},{10,11},{12,13},{14,15},{1,0},{3,2},... | collective-permute-start | bytes 73736 | tf_op jit(solution)/shard_map/ppermute | solution.py:510
  6.3 10.4 %collective-permute-start.1 = (f32[6,8,128]{2,1,0:T(8,128)S(1)}, f32[6,8,128]{2,1,0:T(8,128)S(1)}, u32[]{:S(2)}, u32[]{:S(2)}) collective-permute-start(f32[6,8,128]{2,1,0:T(8,128)S(1)} %get-tuple-element.26.sent_b_ref), channel_id=1, source_target_pairs={{1,2},{3,4},{5,6},{7,8},{9,10},{11,12},{13,14},{15,16},{17,18},{19... | collective-permute-start | bytes 73736 | tf_op jit(solution)/shard_map/ppermute | solution.py:510
  16.7 0.7 %collective-permute-start.2 = (f32[6,8,128]{2,1,0:T(8,128)S(1)}, f32[6,8,128]{2,1,0:T(8,128)S(1)}, u32[]{:S(2)}, u32[]{:S(2)}) collective-permute-start(f32[6,8,128]{2,1,0:T(8,128)S(1)} %get-tuple-element.23.sent_a_ref), channel_id=1, source_target_pairs={{16,17},{18,19},{20,21},{22,23},{24,25},{26,27},{28,29},{30,31},{1... | collective-permute-start | bytes 73736 | tf_op jit(solution)/shard_map/ppermute | solution.py:510
  17.4 0.0 collective-permute-done.early_ref.got_early_ref
  17.4 1.1 %shard_map.65 = (f32[128,14,8,128]{3,2,1,0:T(8,128)S(1)}, f32[2,8,128]{2,1,0:T(8,128)S(1)}) custom-call(f32[64,8,128]{2,1,0:T(8,128)S(1)} %get-tuple-element.20.cx_ref, f32[64,8,128]{2,1,0:T(8,128)S(1)} %get-tuple-element.21.cy_ref, f32[64,8,128]{2,1,0:T(8,128)S(1)} %get-tuple-element.22.vd_ref, s32[1,1]{1,0:T(1,128)S(6)} %copy.7.building_ref, ...), custom_call_target="tpu_custom_call" | custom-call | flops 10000000 | bytes 10000000 | tf_op jit(solution)/shard_map/pallas_call | solution.py:513
  18.6 0.0 collective-permute-done.1.got_b_ref
  18.6 0.0 collective-permute-done.2.got_late_ref
  18.6 1.2 %shard_map.66 = (f32[128,16,128]{2,1,0:T(8,128)S(1)}, f32[128,16,128]{2,1,0:T(8,128)S(1)}, f32[8,8,128]{2,1,0:T(8,128)S(1)}, f32[7,8,128]{2,1,0:T(8,128)S(1)}) custom-call(f32[128,16,128]{2,1,0:T(8,128)S(1)} %get-tuple-element.18.c_ref, f32[64,8,128]{2,1,0:T(8,128)S(1)} %get-tuple-element.19.em_ref, f32[128,14,8,128]{3,2,1,0:T(8,128)S(1)} %get-tuple-element.24.kept_ref, ...), custom_call_target="tpu_custom_call" | custom-call | flops 10000000 | bytes 10000000 | tf_op jit(solution)/shard_map/pallas_call | solution.py:516
  19.7 5.4 %all-gather = f32[28,8,128]{2,1,0:T(8,128)S(1)} all-gather(f32[7,8,128]{2,1,0:T(8,128)S(1)} %get-tuple-element.30), channel_id=2, replica_groups={{0,32,64,96},{128,160,192,224},{256,288,320,352},{384,416,448,480},{1,3..., dimensions={0}, use_global_device_ids=true | all-gather | bytes 143360 | tf_op jit(solution)/shard_map/all_gather | solution.py:523
  25.1 0.2 shard_map.67
  25.3 6.3 %all-gather.1 = f32[14,8,128]{2,1,0:T(8,128)S(1)} all-gather(f32[7,8,128]{2,1,0:T(8,128)S(1)} %shard_map.67), channel_id=3, replica_groups={{0,192},{32,224},{64,128},{96,160},{256,448},{288,480},{320,384},{352,4..., dimensions={0}, use_global_device_ids=true | all-gather | bytes 86016 | tf_op jit(solution)/shard_map/all_gather | solution.py:525
  31.6 0.1 shard_map.68
  31.8 5.7 %all-gather.2 = f32[8,8,128]{2,1,0:T(8,128)S(1)} all-gather(f32[4,8,128]{2,1,0:T(8,128)S(1)} %shard_map.68), channel_id=4, replica_groups={{128,320},{160,352},{192,256},{224,288},{0,448},{32,480},{64,384},{96,4..., dimensions={0}, use_global_device_ids=true | all-gather | bytes 49152 | tf_op jit(solution)/shard_map/all_gather | solution.py:527
  37.5 2.1 %shard_map.69 = f32[128,16,128]{2,1,0:T(8,128)} custom-call(f32[128,16,128]{2,1,0:T(8,128)S(1)} %get-tuple-element.27.side_ref, f32[128,16,128]{2,1,0:T(8,128)S(1)} %get-tuple-element.28.partial_ref, f32[128,14,8,128]{3,2,1,0:T(8,128)S(1)} %get-tuple-element.24.kept_ref, f32[8,8,128]{2,1,0:T(8,128)S(1)} %get-tuple-element.29.ghost_ref, ...), custom_call_target="tpu_custom_call" | custom-call | flops 10000000 | bytes 10000000 | tf_op jit(solution)/shard_map/pallas_call | solution.py:528
Async XLA Ops:
  2.9 14.5 %collective-permute-start = (f32[6,8,128]{2,1,0:T(8,128)S(1)}, f32[6,8,128]{2,1,0:T(8,128)S(1)}, u32[]{:S(2)}, u32[]{:S(2)}) collective-permute-start(f32[6,8,128]{2,1,0:T(8,128)S(1)} %get-tuple-element.23.sent_a_ref), channel_id=1, source_target_pairs={{0,1},{2,3},{4,5},{6,7},{8,9},{10,11},{12,13},{14,15},{1,0},{3,2},... | collective-permute-start | bytes 73736 | tf_op jit(solution)/shard_map/ppermute | solution.py:510
  6.3 12.3 %collective-permute-start.1 = (f32[6,8,128]{2,1,0:T(8,128)S(1)}, f32[6,8,128]{2,1,0:T(8,128)S(1)}, u32[]{:S(2)}, u32[]{:S(2)}) collective-permute-start(f32[6,8,128]{2,1,0:T(8,128)S(1)} %get-tuple-element.26.sent_b_ref), channel_id=1, source_target_pairs={{1,2},{3,4},{5,6},{7,8},{9,10},{11,12},{13,14},{15,16},{17,18},{19... | collective-permute-start | bytes 73736 | tf_op jit(solution)/shard_map/ppermute | solution.py:510
  16.7 1.9 %collective-permute-start.2 = (f32[6,8,128]{2,1,0:T(8,128)S(1)}, f32[6,8,128]{2,1,0:T(8,128)S(1)}, u32[]{:S(2)}, u32[]{:S(2)}) collective-permute-start(f32[6,8,128]{2,1,0:T(8,128)S(1)} %get-tuple-element.23.sent_a_ref), channel_id=1, source_target_pairs={{16,17},{18,19},{20,21},{22,23},{24,25},{26,27},{28,29},{30,31},{1... | collective-permute-start | bytes 73736 | tf_op jit(solution)/shard_map/ppermute | solution.py:510

commit v6 on v5

--- a/solution.py
+++ b/solution.py
@@ -463,14 +463,15 @@
                 out_ref[row, at, :] = far * value + far_low * subs(value, 2) + far_up * subs(value, -2)
                 new_after.append(star)
             after = new_after
-        written(k).start()
+        if k % 2 == 0:
+            written(k // 2).start()
         return after
 
     def written(k):
-        return pltpu.make_async_copy(out_ref.at[pl.ds(8 * k, 8)], out_hbm.at[pl.ds(8 * k, 8)], sems.at[k])
+        return pltpu.make_async_copy(out_ref.at[pl.ds(16 * k, 16)], out_hbm.at[pl.ds(16 * k, 16)], sems.at[k])
 
     stepped(rows, following, PEEL_FINISH)
-    for k in range(16):
+    for k in range(8):
         written(k).wait()
 
 
@@ -531,7 +532,7 @@
         [VMEM] * 7 + [SMEM],
         10**7,
         10**7,
-        scratch=[pltpu.VMEM(field, jnp.float32), pltpu.SemaphoreType.DMA((16,))],
+        scratch=[pltpu.VMEM(field, jnp.float32), pltpu.SemaphoreType.DMA((8,))],
         out_space=HBM,
     )(side, partial, kept, ghost, near, pair, half, building)
     return updated.reshape(concentration.shape)

time: 39.8 us -> 39.8 us (level)
  no operation moved by 1% of the time
where the time goes in v6:
time: 39.8 us; the launch traced here: 39.6 us
  blocking collectives  17.4 us (44%)
  starting transfers between devices  14.5 us (36%)
  Pallas kernels  6.95 us (17%)
  between operations  0.72 us (2%)
    ppermute x3, starting transfers between devices, on_device(): lax.ppermute(sent, 'gy', pairs + [(b, a) for a, b in pairs])  14.5 us
    all_gather x1, blocking collectives, on_device(): pair = lax.all_gather(mine, 'gx', axis_index_groups=pair_groups)  6.34 us
    all_gather x1, blocking collectives, on_device(): half = lax.all_gather(mine, 'gx', axis_index_groups=half_groups)  5.68 us
    all_gather x1, blocking collectives, on_device(): near = lax.all_gather(mine, 'gx', axis_index_groups=near_groups)  5.38 us
    pallas_call x1, Pallas kernels, on_device(): call(pack_kernel, [packed, packed, field] + [x.shape for x in coefs], [HB...  2.24 us
    pallas_call x1, Pallas kernels, on_device(): call(finish_kernel, [field], [VMEM] * 7 + [SMEM], 10 ** 7, 10 ** 7, scrat...  2.09 us
    pallas_call x1, Pallas kernels, on_device(): call(side_kernel, [field, field, (8, SUB, LANE), (7, SUB, LANE)], [VMEM]...  1.16 us
    pallas_call x1, Pallas kernels, on_device(): call(factor_kernel, [(cells, KEPT, SUB, LANE), (2, SUB, LANE)], [VMEM] *...  1.14 us
  transfers between devices with their start and end apart: 3, of which 0 were waited for; matrix products, arithmetic and copies ran while one was open for 0% of the time, Pallas kernels for 3%

profile of v6, /device:TPU:56, one launch (start us, length us, event | category | flops | bytes accessed | tf_op | source)
XLA Modules:
  0.0 39.6 jit_solution(1222179562305775719)
XLA Ops:
  0.7 2.2 %shard_map.64 = (f32[6,8,128]{2,1,0:T(8,128)S(1)}, f32[6,8,128]{2,1,0:T(8,128)S(1)}, f32[128,16,128]{2,1,0:T(8,128)S(1)}, f32[64,8,128]{2,1,0:T(8,128)S(1)}, f32...) custom-call(f32[128,16,128]{2,1,0:T(8,128)} %bitcast.14, f32[64,8,128]{2,1,0:T(8,128)} %bitcast.15, ...), custom_call_target="tpu_custom_call" | custom-call | flops 1000000 | bytes 2000000 | tf_op jit(solution)/shard_map/pallas_call | solution.py:498
  2.9 3.4 %collective-permute-start = (f32[6,8,128]{2,1,0:T(8,128)S(1)}, f32[6,8,128]{2,1,0:T(8,128)S(1)}, u32[]{:S(2)}, u32[]{:S(2)}) collective-permute-start(f32[6,8,128]{2,1,0:T(8,128)S(1)} %get-tuple-element.23.sent_a_ref), channel_id=1, source_target_pairs={{0,1},{2,3},{4,5},{6,7},{8,9},{10,11},{12,13},{14,15},{1,0},{3,2},... | collective-permute-start | bytes 73736 | tf_op jit(solution)/shard_map/ppermute | solution.py:511
  6.3 10.4 %collective-permute-start.1 = (f32[6,8,128]{2,1,0:T(8,128)S(1)}, f32[6,8,128]{2,1,0:T(8,128)S(1)}, u32[]{:S(2)}, u32[]{:S(2)}) collective-permute-start(f32[6,8,128]{2,1,0:T(8,128)S(1)} %get-tuple-element.26.sent_b_ref), channel_id=1, source_target_pairs={{1,2},{3,4},{5,6},{7,8},{9,10},{11,12},{13,14},{15,16},{17,18},{19... | collective-permute-start | bytes 73736 | tf_op jit(solution)/shard_map/ppermute | solution.py:511
  16.7 0.7 %collective-permute-start.2 = (f32[6,8,128]{2,1,0:T(8,128)S(1)}, f32[6,8,128]{2,1,0:T(8,128)S(1)}, u32[]{:S(2)}, u32[]{:S(2)}) collective-permute-start(f32[6,8,128]{2,1,0:T(8,128)S(1)} %get-tuple-element.23.sent_a_ref), channel_id=1, source_target_pairs={{16,17},{18,19},{20,21},{22,23},{24,25},{26,27},{28,29},{30,31},{1... | collective-permute-start | bytes 73736 | tf_op jit(solution)/shard_map/ppermute | solution.py:511
  17.4 0.0 collective-permute-done.early_ref.got_early_ref
  17.4 1.1 %shard_map.65 = (f32[128,14,8,128]{3,2,1,0:T(8,128)S(1)}, f32[2,8,128]{2,1,0:T(8,128)S(1)}) custom-call(f32[64,8,128]{2,1,0:T(8,128)S(1)} %get-tuple-element.20.cx_ref, f32[64,8,128]{2,1,0:T(8,128)S(1)} %get-tuple-element.21.cy_ref, f32[64,8,128]{2,1,0:T(8,128)S(1)} %get-tuple-element.22.vd_ref, s32[1,1]{1,0:T(1,128)S(6)} %copy.7.building_ref, ...), custom_call_target="tpu_custom_call" | custom-call | flops 10000000 | bytes 10000000 | tf_op jit(solution)/shard_map/pallas_call | solution.py:514
  18.6 0.0 collective-permute-done.1.got_b_ref
  18.6 0.0 collective-permute-done.2.got_late_ref
  18.6 1.2 %shard_map.66 = (f32[128,16,128]{2,1,0:T(8,128)S(1)}, f32[128,16,128]{2,1,0:T(8,128)S(1)}, f32[8,8,128]{2,1,0:T(8,128)S(1)}, f32[7,8,128]{2,1,0:T(8,128)S(1)}) custom-call(f32[128,16,128]{2,1,0:T(8,128)S(1)} %get-tuple-element.18.c_ref, f32[64,8,128]{2,1,0:T(8,128)S(1)} %get-tuple-element.19.em_ref, f32[128,14,8,128]{3,2,1,0:T(8,128)S(1)} %get-tuple-element.24.kept_ref, ...), custom_call_target="tpu_custom_call" | custom-call | flops 10000000 | bytes 10000000 | tf_op jit(solution)/shard_map/pallas_call | solution.py:517
  19.7 5.4 %all-gather = f32[28,8,128]{2,1,0:T(8,128)S(1)} all-gather(f32[7,8,128]{2,1,0:T(8,128)S(1)} %get-tuple-element.30), channel_id=2, replica_groups={{0,32,64,96},{128,160,192,224},{256,288,320,352},{384,416,448,480},{1,3..., dimensions={0}, use_global_device_ids=true | all-gather | bytes 143360 | tf_op jit(solution)/shard_map/all_gather | solution.py:524
  25.1 0.2 shard_map.67
  25.3 6.3 %all-gather.1 = f32[14,8,128]{2,1,0:T(8,128)S(1)} all-gather(f32[7,8,128]{2,1,0:T(8,128)S(1)} %shard_map.67), channel_id=3, replica_groups={{0,192},{32,224},{64,128},{96,160},{256,448},{288,480},{320,384},{352,4..., dimensions={0}, use_global_device_ids=true | all-gather | bytes 86016 | tf_op jit(solution)/shard_map/all_gather | solution.py:526
  31.6 0.1 shard_map.68
  31.8 5.7 %all-gather.2 = f32[8,8,128]{2,1,0:T(8,128)S(1)} all-gather(f32[4,8,128]{2,1,0:T(8,128)S(1)} %shard_map.68), channel_id=4, replica_groups={{128,320},{160,352},{192,256},{224,288},{0,448},{32,480},{64,384},{96,4..., dimensions={0}, use_global_device_ids=true | all-gather | bytes 49152 | tf_op jit(solution)/shard_map/all_gather | solution.py:528
  37.5 2.1 %shard_map.69 = f32[128,16,128]{2,1,0:T(8,128)} custom-call(f32[128,16,128]{2,1,0:T(8,128)S(1)} %get-tuple-element.27.side_ref, f32[128,16,128]{2,1,0:T(8,128)S(1)} %get-tuple-element.28.partial_ref, f32[128,14,8,128]{3,2,1,0:T(8,128)S(1)} %get-tuple-element.24.kept_ref, f32[8,8,128]{2,1,0:T(8,128)S(1)} %get-tuple-element.29.ghost_ref, ...), custom_call_target="tpu_custom_call" | custom-call | flops 10000000 | bytes 10000000 | tf_op jit(solution)/shard_map/pallas_call | solution.py:529
Async XLA Ops:
  2.9 14.5 %collective-permute-start = (f32[6,8,128]{2,1,0:T(8,128)S(1)}, f32[6,8,128]{2,1,0:T(8,128)S(1)}, u32[]{:S(2)}, u32[]{:S(2)}) collective-permute-start(f32[6,8,128]{2,1,0:T(8,128)S(1)} %get-tuple-element.23.sent_a_ref), channel_id=1, source_target_pairs={{0,1},{2,3},{4,5},{6,7},{8,9},{10,11},{12,13},{14,15},{1,0},{3,2},... | collective-permute-start | bytes 73736 | tf_op jit(solution)/shard_map/ppermute | solution.py:511
  6.3 12.3 %collective-permute-start.1 = (f32[6,8,128]{2,1,0:T(8,128)S(1)}, f32[6,8,128]{2,1,0:T(8,128)S(1)}, u32[]{:S(2)}, u32[]{:S(2)}) collective-permute-start(f32[6,8,128]{2,1,0:T(8,128)S(1)} %get-tuple-element.26.sent_b_ref), channel_id=1, source_target_pairs={{1,2},{3,4},{5,6},{7,8},{9,10},{11,12},{13,14},{15,16},{17,18},{19... | collective-permute-start | bytes 73736 | tf_op jit(solution)/shard_map/ppermute | solution.py:511
  16.7 1.9 %collective-permute-start.2 = (f32[6,8,128]{2,1,0:T(8,128)S(1)}, f32[6,8,128]{2,1,0:T(8,128)S(1)}, u32[]{:S(2)}, u32[]{:S(2)}) collective-permute-start(f32[6,8,128]{2,1,0:T(8,128)S(1)} %get-tuple-element.23.sent_a_ref), channel_id=1, source_target_pairs={{16,17},{18,19},{20,21},{22,23},{24,25},{26,27},{28,29},{30,31},{1... | collective-permute-start | bytes 73736 | tf_op jit(solution)/shard_map/ppermute | solution.py:511
